TPU v7x, 128 devices: a whole 4x4x4 slice. The times are simulated.
128 devices in a mesh: section: 2 (over x_hi), replica: 4 (over y), shard: 16 (over x_lo, z, core).
Axes of the slice: x: 4 (x_hi: 2, x_lo: 2; x = x_hi * 2 + x_lo), y: 4, z: 4, core: 2. Of those that a mesh axis runs over, the one named last changes fastest.
Arguments:
- inputs: bfloat16 [2, 64, 197, 768], P(None, ('replica', 'shard')), may hold values from -6 to 6
- cotangent: bfloat16 [2, 64, 197, 768], P(None, ('replica', 'shard')), may hold values from -6 to 6
- routes: int32 [2, 2, 64, 197, 2], P('section', None, ('replica', 'shard')), may hold values from 0 to 2, all different within a row
- norm_gain: bfloat16 [2, 2, 768], P('section', None, 'shard'), may hold values from 0.5 to 1.5
- norm_offset: bfloat16 [2, 2, 768], P('section', None, 'shard'), may hold values from -0.5 to 0.5
- w_qkv: bfloat16 [2, 768, 2304], P('section', 'shard'), may hold values from -0.21875 to 0.21875
- w_proj: bfloat16 [2, 768, 768], P('section', 'shard'), may hold values from -3.5 to 3.5
- w_router: bfloat16 [2, 768, 3], P('section', 'shard'), may hold values from -0.15625 to 0.15625
- experts_in: bfloat16 [2, 3072, 3, 768], P('section', 'shard'), may hold values from -0.21875 to 0.21875
- experts_out: bfloat16 [2, 3072, 3, 768], P('section', 'shard'), may hold values from -0.3125 to 0.3125
Outputs:
- section_out: bfloat16 [2, 2, 64, 197, 768], P('section', None, ('replica', 'shard'))
- section_in_grad: float32 [2, 2, 64, 197, 768], P('section', None, ('replica', 'shard'))
- grad_gain: float32 [2, 2, 768], P('section', None, 'shard')
- grad_offset: float32 [2, 2, 768], P('section', None, 'shard')
- grad_qkv: float32 [2, 768, 2304], P('section', 'shard')
- grad_proj: float32 [2, 768, 768], P('section', 'shard')
- grad_router: float32 [2, 768, 3], P('section', 'shard')
- grad_in: float32 [2, 3072, 3, 768], P('section', 'shard')
- grad_out: float32 [2, 3072, 3, 768], P('section', 'shard')
Inputs may be any that keep to these rules, and one draw needn't show every extreme that they name: `routes`: each token names two different experts of the 3, its preferred one first.
All inputs are finite; a program needn't handle non-finite values.
Results may differ from a plain program's by a relative error of at most 0.03.
Values may be sent and summed in bfloat16 or wider, within the bound.
A program may use at most 256 MiB of HBM per device.

v0:
```python
import jax
import jax.numpy as jnp
from jax import lax
from jax.sharding import PartitionSpec as P

HEADS = 12
CAPACITY = 72


EPSILON = 1e-06


def from_behind(value, axis, by):
    peers = lax.axis_size(axis)
    pairs = [(i, i + by) for i in range(peers) if 0 <= i + by < peers]
    return lax.ppermute(value, axis, pairs)


def norm_parts(values, gain_row, offset_row):
    centre = values - jnp.mean(values, axis=-1, keepdims=True)
    rstd_rows = lax.rsqrt(jnp.mean(centre * centre, axis=-1, keepdims=True) + EPSILON)
    scaled = centre * rstd_rows
    return (scaled * gain_row + offset_row, scaled, rstd_rows)


def norm_back(grad_norm, scaled, rstd_rows, gain_row):
    grad_gain = jnp.sum(grad_norm * scaled, axis=(0, 1))
    grad_offset = jnp.sum(grad_norm, axis=(0, 1))
    grad_scaled = grad_norm * gain_row
    grad_values = rstd_rows * (
        grad_scaled
        - jnp.mean(grad_scaled, axis=-1, keepdims=True)
        - scaled * jnp.mean(grad_scaled * scaled, axis=-1, keepdims=True)
    )
    return (grad_values, grad_gain, grad_offset)


def soft_parts(scores):
    largest = jnp.max(scores, axis=-1, keepdims=True)
    expo_rows = jnp.exp(scores - largest)
    row_total = jnp.sum(expo_rows, axis=-1, keepdims=True)
    return (expo_rows / row_total, largest, row_total)


def route_tables(picked_ids, experts):
    picked = jnp.concatenate([picked_ids[:, 0], picked_ids[:, 1]])
    pick_hot = (picked[:, None] == jnp.arange(experts, dtype=jnp.int32)[None, :]).astype(jnp.int32)
    before = jnp.cumsum(pick_hot, axis=0) - pick_hot
    position = jnp.sum(before * pick_hot, axis=1)
    slot_ids = jnp.where(position < CAPACITY, position * experts + picked, CAPACITY * experts)
    slot_table = (
        jnp.arange(CAPACITY * experts, dtype=jnp.int32)[:, None] == slot_ids[None, :]
    ).astype(jnp.bfloat16)
    return (slot_table, pick_hot.astype(jnp.float32), slot_ids)


def expert_forward(slot_in, experts_in, experts_out):
    piece_in = lax.all_gather(experts_in, "shard", axis=0, tiled=True)
    piece_out = lax.all_gather(experts_out, "shard", axis=0, tiled=True)
    pre_part = jnp.einsum("ced,red->cer", slot_in, piece_in, preferred_element_type=jnp.float32)
    hidden = jax.nn.gelu(pre_part).astype(jnp.bfloat16)
    total_out = jnp.einsum("cer,red->ced", hidden, piece_out, preferred_element_type=jnp.float32)
    total_out, pre_all = (total_out, pre_part)
    return (total_out.astype(jnp.bfloat16), (slot_in, pre_all))


def expert_backward(grad_slots, expert_cache, experts_in, experts_out):
    slot_in, pre_all = expert_cache
    piece_in = lax.all_gather(experts_in, "shard", axis=0, tiled=True)
    piece_out = lax.all_gather(experts_out, "shard", axis=0, tiled=True)
    grad_hidden = jnp.einsum(
        "ced,red->cer", grad_slots, piece_out, preferred_element_type=jnp.float32
    )
    unused_value, gelu_back = jax.vjp(jax.nn.gelu, pre_all)
    grad_pre = gelu_back(grad_hidden)[0].astype(jnp.bfloat16)
    total_in = jnp.einsum("cer,red->ced", grad_pre, piece_in, preferred_element_type=jnp.float32)
    total_in, grad_pre_all = (total_in, grad_pre)
    return (total_in, (slot_in, pre_all, grad_slots, grad_pre_all))


def forward_layer(inputs, picked_ids, dense_set, experts_in, experts_out):
    w_qkv, w_proj, w_router, gain_pair, offset_pair = dense_set
    gain_pair = gain_pair.astype(jnp.float32)
    offset_pair = offset_pair.astype(jnp.float32)
    images, length, model_width = inputs.shape
    row_count = images * length
    experts = w_router.shape[1]
    normed_in, scaled_one, rstd_one = norm_parts(inputs, gain_pair[0], offset_pair[0])
    normed_in = normed_in.astype(jnp.bfloat16)
    projected = jnp.einsum(
        "isd,de->ise", normed_in, w_qkv, preferred_element_type=jnp.float32
    ).astype(jnp.bfloat16)
    split_qkv = projected.reshape(images, length, 3, HEADS, model_width // HEADS)
    scores = jnp.einsum(
        "iqhd,ikhd->ihqk",
        split_qkv[:, :, 0],
        split_qkv[:, :, 1],
        preferred_element_type=jnp.float32,
    ) * (model_width // HEADS) ** (-0.5)
    probs_f, largest, row_total = soft_parts(scores)
    mixed_b = (
        jnp.einsum(
            "ihqk,ikhd->iqhd",
            probs_f.astype(jnp.bfloat16),
            split_qkv[:, :, 2],
            preferred_element_type=jnp.float32,
        )
        .astype(jnp.bfloat16)
        .reshape(images, length, model_width)
    )
    residual = inputs + jnp.einsum(
        "isd,de->ise", mixed_b, w_proj, preferred_element_type=jnp.float32
    )
    normed, scaled_two, rstd_two = norm_parts(residual, gain_pair[1], offset_pair[1])
    normed = normed.astype(jnp.bfloat16).reshape(row_count, model_width)
    gate_rows, unused_max, unused_total = soft_parts(
        jnp.dot(normed, w_router, preferred_element_type=jnp.float32)
    )
    slot_table, pick_hot, slot_ids = route_tables(picked_ids.reshape(row_count, 2), experts)
    row_pairs = jnp.concatenate([normed, normed], axis=0)
    slot_in = (
        jnp.dot(slot_table, row_pairs, preferred_element_type=jnp.float32)
        .astype(jnp.bfloat16)
        .reshape(CAPACITY, experts, model_width)
    )
    result, expert_cache = expert_forward(slot_in, experts_in, experts_out)
    combined = jnp.einsum(
        "st,sd->td",
        slot_table,
        result.reshape(CAPACITY * experts, model_width),
        preferred_element_type=jnp.float32,
    )
    gate_first = jnp.sum(gate_rows * pick_hot[:row_count], axis=1)
    gate_second = jnp.sum(gate_rows * pick_hot[row_count:], axis=1)
    expert_sum = (
        combined[:row_count] * gate_first[:, None] + combined[row_count:] * gate_second[:, None]
    )
    output = residual + expert_sum.reshape(images, length, model_width)
    cache_now = (
        scaled_one,
        rstd_one,
        normed_in,
        projected,
        largest,
        row_total,
        mixed_b,
        scaled_two,
        rstd_two,
        normed,
        gate_rows,
        slot_table,
        pick_hot,
        slot_ids,
        combined,
        expert_cache,
    )
    return (output, cache_now)


def backward_layer(grad_y, cache_now, dense_set, experts_in, experts_out):
    w_qkv, w_proj, w_router, gain_pair, offset_pair = dense_set
    gain_pair = gain_pair.astype(jnp.float32)
    (
        scaled_one,
        rstd_one,
        normed_in,
        projected,
        largest,
        row_total,
        mixed_b,
        scaled_two,
        rstd_two,
        normed,
        gate_rows,
        slot_table,
        pick_hot,
        slot_ids,
        combined,
        expert_cache,
    ) = cache_now
    images, length, model_width = grad_y.shape
    row_count = images * length
    head_dim = model_width // HEADS
    experts = w_router.shape[1]
    flat_grad = grad_y.reshape(row_count, model_width)
    gate_first = jnp.sum(gate_rows * pick_hot[:row_count], axis=1)
    gate_second = jnp.sum(gate_rows * pick_hot[row_count:], axis=1)
    grad_combined = jnp.concatenate(
        [flat_grad * gate_first[:, None], flat_grad * gate_second[:, None]], axis=0
    )
    grad_slots = (
        jnp.dot(slot_table, grad_combined.astype(jnp.bfloat16), preferred_element_type=jnp.float32)
        .astype(jnp.bfloat16)
        .reshape(CAPACITY, experts, model_width)
    )
    grad_pick_first = jnp.sum(flat_grad * combined[:row_count], axis=1)
    grad_pick_second = jnp.sum(flat_grad * combined[row_count:], axis=1)
    grad_gates = (
        pick_hot[:row_count] * grad_pick_first[:, None]
        + pick_hot[row_count:] * grad_pick_second[:, None]
    )
    grad_logits = (
        gate_rows * (grad_gates - jnp.sum(grad_gates * gate_rows, axis=1, keepdims=True))
    ).astype(jnp.bfloat16)
    grad_slot_in, expert_part = expert_backward(grad_slots, expert_cache, experts_in, experts_out)
    padded = jnp.concatenate(
        [
            grad_slot_in.reshape(CAPACITY * experts, model_width),
            jnp.zeros((1, model_width), jnp.float32),
        ],
        axis=0,
    )
    taken_rows = padded[slot_ids]
    grad_normed = taken_rows[:row_count] + taken_rows[row_count:]
    grad_router = jnp.einsum("td,te->de", normed, grad_logits, preferred_element_type=jnp.float32)
    grad_normed = grad_normed + jnp.einsum(
        "te,de->td", grad_logits, w_router, preferred_element_type=jnp.float32
    )
    grad_norm_two, grad_gain_two, grad_offset_two = norm_back(
        grad_normed.reshape(images, length, model_width), scaled_two, rstd_two, gain_pair[1]
    )
    grad_residual = grad_y + grad_norm_two
    grad_attn = grad_residual.astype(jnp.bfloat16)
    grad_proj = jnp.einsum("isd,ise->de", mixed_b, grad_attn, preferred_element_type=jnp.float32)
    grad_mixed = (
        jnp.einsum("ise,de->isd", grad_attn, w_proj, preferred_element_type=jnp.float32)
        .astype(jnp.bfloat16)
        .reshape(images, length, HEADS, head_dim)
    )
    split_qkv = projected.reshape(images, length, 3, HEADS, head_dim)
    queries, key_rows, value_rows = (split_qkv[:, :, 0], split_qkv[:, :, 1], split_qkv[:, :, 2])
    scale_at = head_dim ** (-0.5)
    scores = (
        jnp.einsum("iqhd,ikhd->ihqk", queries, key_rows, preferred_element_type=jnp.float32)
        * scale_at
    )
    probs_f = jnp.exp(scores - largest) / row_total
    grad_probs = jnp.einsum(
        "iqhd,ikhd->ihqk", grad_mixed, value_rows, preferred_element_type=jnp.float32
    )
    grad_values = jnp.einsum(
        "ihqk,iqhd->ikhd",
        probs_f.astype(jnp.bfloat16),
        grad_mixed,
        preferred_element_type=jnp.float32,
    )
    grad_scores = (
        probs_f * (grad_probs - jnp.sum(grad_probs * probs_f, axis=-1, keepdims=True))
    ).astype(jnp.bfloat16)
    grad_queries = (
        jnp.einsum("ihqk,ikhd->iqhd", grad_scores, key_rows, preferred_element_type=jnp.float32)
        * scale_at
    )
    grad_keys = (
        jnp.einsum("ihqk,iqhd->ikhd", grad_scores, queries, preferred_element_type=jnp.float32)
        * scale_at
    )
    grad_projected = (
        jnp.stack([grad_queries, grad_keys, grad_values], axis=2)
        .astype(jnp.bfloat16)
        .reshape(images, length, 3 * model_width)
    )
    grad_qkv = jnp.einsum(
        "isd,ise->de", normed_in, grad_projected, preferred_element_type=jnp.float32
    )
    grad_normed_in = jnp.einsum(
        "ise,de->isd", grad_projected, w_qkv, preferred_element_type=jnp.float32
    )
    grad_norm_one, grad_gain_one, grad_offset_one = norm_back(
        grad_normed_in, scaled_one, rstd_one, gain_pair[0]
    )
    grad_inputs = grad_residual + grad_norm_one
    dense_part = (
        grad_qkv,
        grad_proj,
        grad_router,
        jnp.stack([grad_gain_one, grad_gain_two]),
        jnp.stack([grad_offset_one, grad_offset_two]),
    )
    return (grad_inputs, dense_part, expert_part)


def local(
    inputs,
    cotangent,
    routes,
    norm_gain,
    norm_offset,
    w_qkv,
    w_proj,
    w_router,
    experts_in,
    experts_out,
):
    sections = lax.axis_size("section")
    section_at = lax.axis_index("section")
    micros = inputs.shape[0]
    tick_count = micros + sections - 1
    local_in = experts_in[0]
    local_out = experts_out[0]
    dense_set = (
        lax.all_gather(w_qkv[0], "shard", axis=0, tiled=True),
        lax.all_gather(w_proj[0], "shard", axis=0, tiled=True),
        lax.all_gather(w_router[0], "shard", axis=0, tiled=True),
        lax.all_gather(norm_gain[0], "shard", axis=1, tiled=True),
        lax.all_gather(norm_offset[0], "shard", axis=1, tiled=True),
    )
    received = jnp.zeros(inputs.shape[1:], jnp.bfloat16)
    outputs = []
    caches = []
    for tick_at in range(tick_count):
        micro_at = jnp.clip(tick_at - section_at, 0, micros - 1)
        fresh_in = lax.dynamic_index_in_dim(inputs, micro_at, 0, keepdims=False)
        current = jnp.where(section_at == 0, fresh_in, received)
        picked = lax.dynamic_index_in_dim(routes[0], micro_at, 0, keepdims=False)
        result, cache_now = forward_layer(
            current.astype(jnp.float32), picked, dense_set, local_in, local_out
        )
        sent_out = result.astype(jnp.bfloat16)
        outputs.append(sent_out)
        caches.append(cache_now)
        if tick_at + 1 < tick_count:
            received = from_behind(sent_out, "section", 1)
    section_out = lax.dynamic_slice_in_dim(jnp.stack(outputs), section_at, micros, 0)[None]
    stacked_cache = jax.tree.map(lambda *items: jnp.stack(items), *caches)
    dense_again = (
        lax.all_gather(w_qkv[0], "shard", axis=0, tiled=True),
        lax.all_gather(w_proj[0], "shard", axis=0, tiled=True),
        lax.all_gather(w_router[0], "shard", axis=0, tiled=True),
        lax.all_gather(norm_gain[0], "shard", axis=1, tiled=True),
        lax.all_gather(norm_offset[0], "shard", axis=1, tiled=True),
    )
    returned = jnp.zeros(inputs.shape[1:], jnp.bfloat16)
    grad_list = []
    expert_list = []
    dense_sums = None
    for tick_at in range(tick_count):
        offset_at = tick_at - (sections - 1 - section_at)
        micro_at = jnp.clip(offset_at, 0, micros - 1)
        is_valid = (offset_at >= 0) & (offset_at < micros)
        cache_now = jax.tree.map(
            lambda item: lax.dynamic_index_in_dim(item, micro_at + section_at, 0, keepdims=False),
            stacked_cache,
        )
        given_grad = lax.dynamic_index_in_dim(cotangent, micro_at, 0, keepdims=False).astype(
            jnp.float32
        )
        grad_y = jnp.where(section_at == sections - 1, given_grad, returned.astype(jnp.float32))
        grad_y = jnp.where(is_valid, grad_y, 0.0)
        grad_inputs, dense_part, expert_part = backward_layer(
            grad_y, cache_now, dense_again, local_in, local_out
        )
        dense_sums = (
            dense_part if dense_sums is None else jax.tree.map(jnp.add, dense_sums, dense_part)
        )
        expert_list.append(expert_part)
        grad_list.append(grad_inputs)
        if tick_at + 1 < tick_count:
            returned = from_behind(grad_inputs.astype(jnp.bfloat16), "section", -1)
    section_in_grad = lax.dynamic_slice_in_dim(
        jnp.stack(grad_list), sections - 1 - section_at, micros, 0
    )[None]
    sum_qkv, sum_proj, sum_router, sum_gain, sum_offset = dense_sums
    shard_qkv, shard_proj, shard_router, shard_gain, shard_offset = (
        lax.psum_scatter(
            sum_qkv.astype(jnp.bfloat16), "shard", scatter_dimension=0, tiled=True
        ).astype(jnp.float32),
        lax.psum_scatter(
            sum_proj.astype(jnp.bfloat16), "shard", scatter_dimension=0, tiled=True
        ).astype(jnp.float32),
        lax.psum_scatter(
            sum_router.astype(jnp.bfloat16), "shard", scatter_dimension=0, tiled=True
        ).astype(jnp.float32),
        lax.psum_scatter(
            sum_gain.astype(jnp.bfloat16), "shard", scatter_dimension=1, tiled=True
        ).astype(jnp.float32),
        lax.psum_scatter(
            sum_offset.astype(jnp.bfloat16), "shard", scatter_dimension=1, tiled=True
        ).astype(jnp.float32),
    )
    slot_ins, pre_alls, grad_slot_rows, grad_pres = jax.tree.map(
        lambda *items: jnp.stack(items), *expert_list
    )
    hidden = jax.nn.gelu(pre_alls).astype(jnp.bfloat16)
    grad_first = jnp.einsum(
        "tced,tcer->red", slot_ins, grad_pres, preferred_element_type=jnp.float32
    )
    grad_second = jnp.einsum(
        "tcer,tced->red", hidden, grad_slot_rows, preferred_element_type=jnp.float32
    )
    expert_grads = lax.psum_scatter(
        jnp.stack([grad_first, grad_second], axis=1).astype(jnp.bfloat16),
        "shard",
        scatter_dimension=0,
        tiled=True,
    )
    total_qkv, total_proj, total_router, total_gain, total_offset, total_expert = (
        lax.psum(shard_qkv.astype(jnp.bfloat16), "replica").astype(jnp.float32),
        lax.psum(shard_proj.astype(jnp.bfloat16), "replica").astype(jnp.float32),
        lax.psum(shard_router.astype(jnp.bfloat16), "replica").astype(jnp.float32),
        lax.psum(shard_gain.astype(jnp.bfloat16), "replica").astype(jnp.float32),
        lax.psum(shard_offset.astype(jnp.bfloat16), "replica").astype(jnp.float32),
        lax.psum(expert_grads, "replica").astype(jnp.float32),
    )
    return (
        section_out,
        section_in_grad,
        total_gain[None],
        total_offset[None],
        total_qkv[None],
        total_proj[None],
        total_router[None],
        total_expert[:, 0][None],
        total_expert[:, 1][None],
    )


def solution(mesh):
    return jax.shard_map(
        local,
        mesh=mesh,
        in_specs=(
            P(None, ("replica", "shard"), None, None),
            P(None, ("replica", "shard"), None, None),
            P("section", None, ("replica", "shard"), None, None),
            P("section", None, "shard"),
            P("section", None, "shard"),
            P("section", "shard", None),
            P("section", "shard", None),
            P("section", "shard", None),
            P("section", "shard", None, None),
            P("section", "shard", None, None),
        ),
        out_specs=(
            P("section", None, ("replica", "shard"), None, None),
            P("section", None, ("replica", "shard"), None, None),
            P("section", None, "shard"),
            P("section", None, "shard"),
            P("section", "shard", None),
            P("section", "shard", None),
            P("section", "shard", None),
            P("section", "shard", None, None),
            P("section", "shard", None, None),
        ),
        check_vma=False,
    )
```

profile of v0, /device:TPU:1, one launch (start us, length us, event | category | flops | bytes accessed | tf_op | source)
XLA Modules:
  0.0 1070.9 jit_solution(4975297025502793277)
XLA Ops:
  10.9 24.0 %all-gather.1 = bf16[1,2,768]{1,0,2:T(2,128)(2,1)S(1)} all-gather(bf16[1,2,48]{1,0,2:T(2,128)(2,1)S(1)} %copy.172), channel_id=3, replica_groups=mesh['section'=2,'replica'=4,'shard'=16] {'shard'}, dimensions={2}, use_global_device_ids=true | all-gather | bytes 3264 | tf_op jit(solution)/shard_map/all_gather | solution.py:306
  35.4 17.7 %all-gather = bf16[1,2,768]{1,0,2:T(2,128)(2,1)S(1)} all-gather(bf16[1,2,48]{1,0,2:T(2,128)(2,1)S(1)} %copy.171), channel_id=2, replica_groups=mesh['section'=2,'replica'=4,'shard'=16] {'shard'}, dimensions={2}, use_global_device_ids=true | all-gather | bytes 3264 | tf_op jit(solution)/shard_map/all_gather | solution.py:305
  55.2 19.4 %all-gather.6 = bf16[1,768,3]{2,0,1:T(2,128)(2,1)S(1)} all-gather(bf16[1,48,3]{2,0,1:T(2,128)(2,1)S(1)} %copy.177), channel_id=8, replica_groups=mesh['section'=2,'replica'=4,'shard'=16] {'shard'}, dimensions={1}, use_global_device_ids=true | all-gather | bytes 4896 | tf_op jit(solution)/shard_map/all_gather | solution.py:304
  107.2 59.9 %all-gather.16.cloned.1.call-done = bf16[1,3072,3,768]{3,1,2,0:T(8,128)(2,1)} async-done(((bf16[1,192,3,768]{3,1,2,0:T(8,128)(2,1)}), bf16[1,3072,3,768]{3,1,2,0:T(8,128)(2,1)}) %all-gather.16.cloned.1.call-update) | async-done | bytes 14155792 | tf_op jit(solution)/shard_map/all_gather | solution.py:58
  167.1 9.5 fusion.24
  176.6 72.3 %all-gather.18.cloned.1.call-done = bf16[1,3072,3,768]{3,1,2,0:T(8,128)(2,1)} async-done(((bf16[1,192,3,768]{3,1,2,0:T(8,128)(2,1)}), bf16[1,3072,3,768]{3,1,2,0:T(8,128)(2,1)}) %all-gather.18.cloned.1.call-update) | async-done | bytes 14155792 | tf_op jit(solution)/shard_map/all_gather | solution.py:59
  281.7 9.5 fusion.22
  291.2 8.8 fusion.176
  333.7 9.4 fusion.20
  343.1 8.8 fusion.171
  366.6 10.3 fusion.64
  437.9 10.5 fusion.71
  494.6 10.3 fusion.78
  504.9 7.9 fusion.145
  566.9 10.5 fusion
  577.4 10.1 fusion.1
  587.5 20.1 %pad_maximum_fusion = bf16[3072,2,3,768]{3,0,2,1:T(8,128)(2,1)} fusion(bf16[3072,1,3,768]{3,0,2,1:T(8,128)(2,1)} %fusion.1, bf16[3072,1,3,768]{3,0,2,1:T(8,128)(2,1)} %fusion), kind=kLoop, calls=%fused_computation.3 | loop fusion | flops 14155776 | bytes 56623104 | tf_op jit(solution)/shard_map/stack | solution.py:392
  619.3 32.3 %reduce-scatter.13.cloned.1.call-done = bf16[48,2304]{1,0:T(8,128)(2,1)} async-done(((bf16[768,2304]{1,0:T(8,128)(2,1)}), bf16[48,2304]{1,0:T(8,128)(2,1)}) %reduce-scatter.13.cloned.1.call-update) | async-done | bytes 221200 | tf_op jit(solution)/shard_map/reduce_scatter | solution.py:365
  651.6 160.0 %reduce-scatter.17.cloned.1.call-done = bf16[192,2,3,768]{3,0,2,1:T(8,128)(2,1)} async-done(((bf16[3072,2,3,768]{3,0,2,1:T(8,128)(2,1)}), bf16[192,2,3,768]{3,0,2,1:T(8,128)(2,1)}) %reduce-scatter.17.cloned.1.call-update) | async-done | bytes 1769488 | tf_op jit(solution)/shard_map/reduce_scatter | solution.py:391
  818.3 52.4 %reduce-scatter.19.cloned.1.call-done = bf16[48,2]{1,0:T(8,128)(2,1)} async-done(((bf16[768,2]{1,0:T(8,128)(2,1)}), bf16[48,2]{1,0:T(8,128)(2,1)}) %reduce-scatter.19.cloned.1.call-update) | async-done | bytes 208
  871.5 60.5 %reduce-scatter.21.cloned.1.call-done = bf16[48,2]{1,0:T(8,128)(2,1)} async-done(((bf16[768,2]{1,0:T(8,128)(2,1)}), bf16[48,2]{1,0:T(8,128)(2,1)}) %reduce-scatter.21.cloned.1.call-update) | async-done | bytes 208
  932.8 60.6 %reduce-scatter.23.cloned.1.call-done = bf16[48,3]{1,0:T(8,128)(2,1)} async-done(((bf16[768,3]{1,0:T(8,128)(2,1)}), bf16[48,3]{1,0:T(8,128)(2,1)}) %reduce-scatter.23.cloned.1.call-update) | async-done | bytes 304
  994.2 8.6 all-reduce.6
  1004.6 52.5 %all-reduce.10.cloned.1.call-done = (bf16[1,48,2304]{2,1,0:T(8,128)(2,1)}, bf16[1,48,768]{2,1,0:T(8,128)(2,1)}, bf16[192,2,3,768]{3,0,2,1:T(8,128)(2,1)}) async-done(((bf16[1,48,2304]{2,1,0:T(8,128)(2,1)}, bf16[1,48,768]{2,1,0:T(8,128)(2,1)}, bf16[192,2,3,768]{3,0,2,1:T(8,128)(2,1)}), (bf16[1,48,2304]{2,1,0:T(8,128)(2,1)}, bf16[1,48,768]{2,1,0:T(8,128)(2,1)}, ...) | async-done | bytes 2064400 | tf_op jit(solution)/shard_map/psum | solution.py:398
  (632 shorter events, 308.4 us)
Async XLA Ops:
  7.2 47.9 %copy-start.143 = (bf16[1,48,3]{1,2,0:T(4,128)(2,1)S(1)}, bf16[1,48,3]{1,2,0:T(4,128)(2,1)}, u32[]{:S(2)}) copy-start(bf16[1,48,3]{1,2,0:T(4,128)(2,1)} %param.17) | copy-start | bytes 868
  7.2 89.6 %all-gather.12.cloned.1.call-start = ((), (), s32[]{:S(2)}) async-start(), calls=%async_computation.9 | async-start | bytes 3760128 | tf_op jit(solution)/shard_map/all_gather | solution.py:302
  7.9 94.4 %all-gather.14.cloned.1.call-start = ((), (), s32[]{:S(2)}) async-start(), calls=%async_computation.10 | async-start | bytes 1253376 | tf_op jit(solution)/shard_map/all_gather | solution.py:303
  8.7 158.4 %all-gather.16.cloned.1.call-start = ((), (), s32[]{:S(2)}) async-start(), calls=%async_computation.11 | async-start | bytes 15040512 | tf_op jit(solution)/shard_map/all_gather | solution.py:58
  9.4 239.5 %all-gather.18.cloned.1.call-start = ((), (), s32[]{:S(2)}) async-start(), calls=%async_computation.12 | async-start | bytes 15040512 | tf_op jit(solution)/shard_map/all_gather | solution.py:59
  10.0 609.3 %reduce-scatter.15.cloned.1.call-start = ((), (), s32[]{:S(2)}) async-start(), calls=%async_computation.7 | async-start | bytes 1253376 | tf_op jit(solution)/shard_map/reduce_scatter | solution.py:368
  10.1 70.9 %copy-start.20 = (bf16[2,1,197,768]{3,0,2,1:T(2,128)(2,1)S(1)}, bf16[2,1,197,768]{3,0,2,1:T(2,128)(2,1)}, u32[]{:S(2)}) copy-start(bf16[2,1,197,768]{3,0,2,1:T(2,128)(2,1)} %param.10) | copy-start | bytes 1815556
  79.9 354.3 %copy-start.77 = (f32[3,394,3]{1,2,0:T(4,128)}, f32[3,394,3]{1,2,0:T(4,128)S(1)}, u32[]{:S(2)}) copy-start(f32[3,394,3]{1,2,0:T(4,128)S(1)} %pad_maximum_fusion.11) | copy-start | bytes 42556
  176.6 80.0 %copy-start.6 = (f32[3,72,3072]{2,1,0:T(8,128)}, f32[3,72,3072]{2,1,0:T(8,128)S(1)}, u32[]{:S(2)}) copy-start(f32[3,72,3072]{2,1,0:T(8,128)S(1)} %fusion.24) | copy-start | bytes 7962628
  259.6 11.2 %collective-permute-start = (bf16[1,197,768]{2,1,0:T(8,128)(2,1)S(1)}, bf16[1,197,768]{2,1,0:T(8,128)(2,1)S(1)}, u32[]{:S(2)}, u32[]{:S(2)}) collective-permute-start(bf16[1,197,768]{2,1,0:T(8,128)(2,1)S(1)} %bitcast.1042), channel_id=1, source_target_pairs={{0,64},{1,65},{2,66},{3,67},{4,68},{5,69},{6,70},{7,71},{8,72},{9,... | collective-permute-start | bytes 907784 | tf_op jit(solution)/shard_map/ppermute | solution.py:16
  306.3 11.6 %collective-permute-start.1 = (bf16[1,197,768]{2,1,0:T(8,128)(2,1)}, bf16[1,197,768]{2,1,0:T(8,128)(2,1)S(1)}, u32[]{:S(2)}, u32[]{:S(2)}) collective-permute-start(bf16[1,197,768]{2,1,0:T(8,128)(2,1)} %fusion.248), channel_id=1, source_target_pairs={{0,64},{1,65},{2,66},{3,67},{4,68},{5,69},{6,70},{7,71},{8,72},{9,... | collective-permute-start | bytes 907784 | tf_op jit(solution)/shard_map/ppermute | solution.py:16
  414.5 18.0 %collective-permute-start.2 = (bf16[1,197,768]{2,1,0:T(8,128)(2,1)}, bf16[1,197,768]{2,1,0:T(8,128)(2,1)S(1)}, u32[]{:S(2)}, u32[]{:S(2)}) collective-permute-start(bf16[1,197,768]{2,1,0:T(8,128)(2,1)} %get-tuple-element.104), channel_id=1, source_target_pairs={{64,0},{65,1},{66,2},{67,3},{68,4},{69,5},{70,6},{71,7},{72,8},{73... | collective-permute-start | bytes 907784 | tf_op jit(solution)/shard_map/ppermute | solution.py:16
  480.1 10.4 collective-permute-start.3
  524.5 127.1 %reduce-scatter.13.cloned.1.call-start = ((), (), s32[]{:S(2)}) async-start(), calls=%async_computation.6 | async-start | bytes 3760128 | tf_op jit(solution)/shard_map/reduce_scatter | solution.py:365
  541.8 269.8 %reduce-scatter.17.cloned.1.call-start = ((), (), s32[]{:S(2)}) async-start(), calls=%async_computation.8 | async-start | bytes 30081024 | tf_op jit(solution)/shard_map/reduce_scatter | solution.py:391
  607.7 263.0 %reduce-scatter.19.cloned.1.call-start = ((), (), s32[]{:S(2)}) async-start(), calls=%async_computation.13 | async-start | bytes 208896
  615.0 196.6 %copy-start.10 = (f32[394,768]{1,0:T(8,128)S(1)}, f32[394,768]{1,0:T(8,128)}, u32[]{:S(2)}) copy-start(f32[394,768]{1,0:T(8,128)} %copy-done.9) | copy-start | bytes 3631108
  615.0 196.6 %copy-start.14 = (f32[1,197,768]{2,1,0:T(8,128)S(1)}, f32[1,197,768]{2,1,0:T(8,128)}, u32[]{:S(2)}) copy-start(f32[1,197,768]{2,1,0:T(8,128)} %copy-done.13) | copy-start | bytes 1815556
  615.0 196.6 %copy-start.124 = (f32[197]{0:T(256)S(1)}, f32[197]{0:T(256)}, u32[]{:S(2)}) copy-start(f32[197]{0:T(256)} %get-tuple-element.88) | copy-start | bytes 2368
  615.0 196.6 %copy-start.125 = (f32[197]{0:T(256)S(1)}, f32[197]{0:T(256)}, u32[]{:S(2)}) copy-start(f32[197]{0:T(256)} %get-tuple-element.89) | copy-start | bytes 2368
  615.9 316.1 %reduce-scatter.21.cloned.1.call-start = ((), (), s32[]{:S(2)}) async-start(), calls=%async_computation.14 | async-start | bytes 208896
  616.8 195.0 %copy-start.74 = (bf16[197,768]{1,0:T(8,128)(2,1)S(1)}, bf16[197,768]{1,0:T(8,128)(2,1)}, u32[]{:S(2)}) copy-start(bf16[197,768]{1,0:T(8,128)(2,1)} %copy-done.73) | copy-start | bytes 907780
  616.9 376.6 %reduce-scatter.23.cloned.1.call-start = ((), (), s32[]{:S(2)}) async-start(), calls=%async_computation.15 | async-start | bytes 208896
  619.0 438.1 %all-reduce.10.cloned.1.call-start = ((), (), s32[]{:S(2)}) async-start(), calls=%async_computation.16 | async-start | bytes 4128768 | tf_op jit(solution)/shard_map/psum | solution.py:398
  (144 other events, 733.6 us)
Sparse Core Ops, SparseCore 0:
  9.7 41.2 all-gather.11
  52.7 33.1 all-gather.13
  87.6 79.4 all-gather.15
  168.6 80.2 all-gather.17
  524.6 60.4 reduce-scatter.14
  587.4 64.1 reduce-scatter.12
  654.0 157.5 reduce-scatter.16
  813.9 56.7 reduce-scatter.18
  873.2 58.7 reduce-scatter.20
  934.8 58.6 reduce-scatter.22
  996.2 60.8 all-reduce.9
where the time goes:
time: 1080 us; the launch traced here: 1070 us
  waiting for transfers between devices  564 us (52%)
  matrix products  210 us (19%)
  local copies, waits for them, and re-layouts  117 us (11%)
  other arithmetic  78.7 us (7%)
  blocking collectives  69.7 us (6%)
  between operations  16.7 us (2%)
  starting transfers between devices  13.9 us (1%)
    unnamed x14, waiting for transfers between devices  176 us
    reduce_scatter x1, waiting for transfers between devices, local(): lax.psum_scatter(jnp.stack([grad_first, grad_second], axis=1).astype(jnp....  160 us
    all_gather x1, waiting for transfers between devices, expert_forward(): piece_out = lax.all_gather(experts_out, 'shard', axis=0, tiled=True)  72.3 us
    all_gather x1, waiting for transfers between devices, expert_forward(): piece_in = lax.all_gather(experts_in, 'shard', axis=0, tiled=True)  59.9 us
    psum x1, waiting for transfers between devices, local(): lax.psum(shard_qkv.astype(jnp.bfloat16), 'replica').astype(jnp.float32)  52.5 us
    reduce_scatter x1, waiting for transfers between devices, local(): lax.psum_scatter(sum_qkv.astype(jnp.bfloat16), 'shard', scatter_dimension...  32.3 us
    dot_general x3, matrix products, expert_backward(): jnp.einsum('ced,red->cer', grad_slots, piece_out, preferred_element_type=...  31 us
    unnamed x323, local copies, waits for them, and re-layouts  28.9 us
  transfers between devices with their start and end apart: 15, of which 11 were waited for; matrix products, arithmetic and copies ran while one was open for 16% of the time, Pallas kernels for 0%

commit v1 on v0

v1 whole, which is shorter than its diff:
```python
import jax
import jax.numpy as jnp
from jax import lax
from jax.experimental import pallas as pl
from jax.experimental.pallas import tpu as pltpu
from jax.sharding import PartitionSpec as P

MESH = pl.DeviceIdType.MESH

def place():
    j = lax.axis_index("shard")
    return j // 8, (j // 2) % 4, j % 2, lax.axis_index("replica")

def at_shard(xl, z, c):
    return {"shard": xl * 8 + z * 2 + c}

class Copies:
    def __init__(self, send, recv):
        self.send, self.recv, self.n, self.all = send, recv, 0, []
    def __call__(self, src, dst, dev):
        cp = pltpu.make_async_remote_copy(src_ref=src, dst_ref=dst, send_sem=self.send.at[self.n], recv_sem=self.recv.at[self.n], device_id=dev, device_id_type=MESH)
        self.n += 1
        cp.start()
        self.all.append(cp)
        return cp

def greet(devs):
    b = pltpu.get_barrier_semaphore()
    for d in devs:
        pl.semaphore_signal(b, inc=1, device_id=d, device_id_type=MESH)
    pl.semaphore_wait(b, len(devs))

def halves(n):
    half = n // 32 * 16
    return (half, n - half)


def gather_kernel(p_rows, q_rows, core, own, out, send, recv, loc):
    xl, z, c, y = place()
    ox, zu, zd, zo = 1 - xl, (z + 1) % 4, (z + 3) % 4, (z + 2) % 4
    yu, yd, yo = (y + 1) % 4, (y + 3) % 4, (y + 2) % 4
    dx, du, dd, dc = at_shard(ox, z, c), at_shard(xl, zu, c), at_shard(xl, zd, c), at_shard(xl, z, 1 - c)
    dyu, dyd = {"replica": yu}, {"replica": yd}
    greet([dx, du, dd, dyu, dyd] + ([dc] if core else []))
    go = Copies(send, recv)
    n = q_rows // 4
    def quarter(k):
        return pl.ds(pl.multiple_of(p_rows + k * n, 16), n)
    def lower(k):
        return pl.ds(pl.multiple_of(p_rows + k * n, 16), halves(n)[0])
    def upper(k):
        return pl.ds(pl.multiple_of(p_rows + k * n + halves(n)[0], 16), halves(n)[1])
    def block(a, b, rows):
        return out.at[a, b, c, rows]
    def pass_on(a, b, rows, dev):
        return go(block(a, b, rows), block(a, b, rows), dev)
    cores = []
    def share(a, b, rows):
        if core:
            cores.append(pass_on(a, b, rows, dc))
    local = pltpu.make_async_copy(own, out.at[xl, z, c], loc)
    local.start()
    mine = quarter(y)
    first = pl.ds(0, p_rows)
    plo, pup = pl.ds(0, halves(p_rows)[0]), pl.ds(halves(p_rows)[0], halves(p_rows)[1])
    def from_own(rows, dev):
        return go(own.at[rows], block(xl, z, rows), dev)
    q_up, q_down, q_over = from_own(mine, du), from_own(mine, dd), from_own(mine, dx)
    p_over = from_own(first, dx)
    p_up, p_down = from_own(first, du), from_own(first, dd)
    q_over.wait_recv()
    q_over_up, q_over_down = pass_on(ox, z, mine, du), pass_on(ox, z, mine, dd)
    spread = []
    def over_y(a, b):
        spread.append((a, b, pass_on(a, b, mine, dyu), pass_on(a, b, mine, dyd)))
    q_up.wait_recv()
    f1 = pass_on(xl, zd, lower(y), du)
    over_y(xl, zd)
    q_down.wait_recv()
    f2 = pass_on(xl, zu, upper(y), dd)
    over_y(xl, zu)
    if core:
        cores.append(go(own, out.at[xl, z, c], dc))
    rest_over = [from_own(quarter(k), dx) for k in (yu, yd, yo)]
    q_over_up.wait_recv()
    f3 = pass_on(ox, zd, lower(y), du)
    over_y(ox, zd)
    q_over_down.wait_recv()
    f4 = pass_on(ox, zu, upper(y), dd)
    over_y(ox, zu)
    p_over.wait_recv()
    p_over_up, p_over_down = pass_on(ox, z, first, du), pass_on(ox, z, first, dd)
    f1.wait_recv()
    f2.wait_recv()
    over_y(xl, zo)
    f3.wait_recv()
    f4.wait_recv()
    over_y(ox, zo)
    for a, b in ((xl, zd), (xl, zu), (ox, zd), (ox, zu), (xl, zo), (ox, zo)):
        share(a, b, mine)
    p_up.wait_recv()
    g1 = pass_on(xl, zd, plo, du)
    p_down.wait_recv()
    g2 = pass_on(xl, zu, pup, dd)
    share(xl, zd, first)
    share(xl, zu, first)
    fy = []
    def y_forward(item):
        a, b, up, down = item
        up.wait_recv()
        one = pass_on(a, b, lower(yd), dyu)
        share(a, b, quarter(yd))
        down.wait_recv()
        two = pass_on(a, b, upper(yu), dyd)
        share(a, b, quarter(yu))
        fy.append((a, b, one, two))
    for item in spread[:2]:
        y_forward(item)
    p_over_up.wait_recv()
    g3 = pass_on(ox, zd, plo, du)
    p_over_down.wait_recv()
    g4 = pass_on(ox, zu, pup, dd)
    share(ox, zd, first)
    share(ox, zu, first)
    for item in spread[2:]:
        y_forward(item)
    for cp in rest_over:
        cp.wait_recv()
    share(ox, z, pl.ds(0, p_rows + q_rows))
    for cp in (g1, g2, g3, g4):
        cp.wait_recv()
    share(xl, zo, first)
    share(ox, zo, first)
    for a, b, one, two in fy:
        one.wait_recv()
        two.wait_recv()
        share(a, b, quarter(yo))
    local.wait()
    for cp in cores:
        cp.wait_recv()
    for cp in go.all:
        cp.wait_send()


def gather(own, p_rows, core=True, cid=0):
    r, w = own.shape
    nmax = 80
    def body(own_ref, out_ref, send, recv, loc):
        gather_kernel(p_rows, r - p_rows, core, own_ref, out_ref, send, recv, loc)
    return pl.pallas_call(
        body,
        out_shape=jax.ShapeDtypeStruct((2, 4, 2, r, w), own.dtype),
        in_specs=[pl.BlockSpec(memory_space=pl.ANY)],
        out_specs=pl.BlockSpec(memory_space=pl.ANY),
        scratch_shapes=[pltpu.SemaphoreType.DMA((nmax,)), pltpu.SemaphoreType.DMA((nmax,)), pltpu.SemaphoreType.DMA(())],
        compiler_params=pltpu.CompilerParams(collective_id=cid, has_side_effects=True),
    )(own)


def reduce_kernel(gexp, gden, out, acc, rc, ryh, ryf, rzh, rzf, rx, rfh, rff, small, send, recv, loc):
    xl, z, c, y = place()
    ox, zu, zd, zo = 1 - xl, (z + 1) % 4, (z + 3) % 4, (z + 2) % 4
    yu, yd, yo = (y + 1) % 4, (y + 3) % 4, (y + 2) % 4
    dx, du, dd, dc = at_shard(ox, z, c), at_shard(xl, zu, c), at_shard(xl, zd, c), at_shard(xl, z, 1 - c)
    dyu, dyd, dyo = {"replica": yu}, {"replica": yd}, {"replica": yo}
    greet([dx, du, dd, dc, dyu, dyd, dyo])
    go = Copies(send, recv)
    locals_ = []

    def load(src, dst):
        cp = pltpu.make_async_copy(src, dst, loc.at[len(locals_)])
        cp.start()
        locals_.append(cp)
        return cp

    def add(dst, dst_at, src, src_at, n):
        def body(i, carry):
            rows = pl.ds(pl.multiple_of(dst_at + i * 16, 16), 16)
            more = pl.ds(pl.multiple_of(src_at + i * 16, 16), 16)
            dst[rows] = dst[rows] + src[more]
            return carry
        lax.fori_loop(0, n // 16, body, 0)

    blocks = [(ox, zo), (xl, zo), (ox, zu), (xl, zu), (ox, zd), (xl, zd), (ox, z), (xl, z)]
    exp_rows, den_rows = pl.ds(0, 384), pl.ds(384, 80)
    parts = []
    for a, b in blocks:
        parts.append((
            load(gexp.at[a, b, c], acc.at[a, b, exp_rows]),
            load(gden.at[a, b, c], acc.at[a, b, den_rows]),
            go(gexp.at[a, b, 1 - c], rc.at[a, b, exp_rows], dc),
            go(gden.at[a, b, 1 - c], rc.at[a, b, den_rows], dc),
        ))

    def own_sum(t):
        a, b = blocks[t]
        one, two, three, four = parts[t]
        one.wait()
        two.wait()
        three.wait_recv()
        four.wait_recv()
        add(acc.at[a, b], 0, rc.at[a, b], 0, 464)

    def quarter(k):
        return 208 + k * 64

    def rows(at, n):
        return pl.ds(pl.multiple_of(at, 16), n)

    def piece(t, at, n):
        a, b = blocks[t]
        return acc.at[a, b, rows(at, n)]

    y_half, y_full, z_half, z_full = {}, {}, {}, {}
    for t in range(6):
        own_sum(t)
        y_half[t] = (
            go(piece(t, quarter(yo), 32), ryh.at[t, 0], dyu),
            go(piece(t, quarter(yo) + 32, 32), ryh.at[t, 1], dyd),
        )
        if t < 2:
            z_half[t, 0] = (
                go(piece(t, 0, 96), rzh.at[t, 0, pl.ds(0, 96)], du),
                go(piece(t, 96, 112), rzh.at[t, 1, pl.ds(0, 112)], dd),
            )
    for t in range(6):
        a, b = blocks[t]
        y_half[t][0].wait_recv()
        add(acc.at[a, b], quarter(yu), ryh.at[t, 0], 0, 32)
        y_full_up = go(piece(t, quarter(yu), 64), ryf.at[t, 0], dyu)
        y_half[t][1].wait_recv()
        add(acc.at[a, b], quarter(yd) + 32, ryh.at[t, 1], 0, 32)
        y_full[t] = (y_full_up, go(piece(t, quarter(yd), 64), ryf.at[t, 1], dyd))
        if t == 1:
            for x in range(2):
                z_half[x, 0][0].wait_recv()
                add(acc.at[blocks[x][0], zu], 0, rzh.at[x, 0], 0, 96)
                up = go(piece(2 + x, 0, 208), rzf.at[x, 0, pl.ds(0, 208)], du)
                z_half[x, 0][1].wait_recv()
                add(acc.at[blocks[x][0], zd], 96, rzh.at[x, 1], 0, 112)
                z_full[x, 0] = (up, go(piece(4 + x, 0, 208), rzf.at[x, 1, pl.ds(0, 208)], dd))
    own_sum(6)
    own_sum(7)
    for t in range(6):
        a, b = blocks[t]
        for side in range(2):
            y_full[t][side].wait_recv()
            add(acc.at[a, b], quarter(y), ryf.at[t, side], 0, 64)
        if t < 2:
            z_half[t, 1] = (
                go(piece(t, quarter(y), 32), rzh.at[t, 0, pl.ds(112, 32)], du),
                go(piece(t, quarter(y) + 32, 32), rzh.at[t, 1, pl.ds(112, 32)], dd),
            )
    over = []
    for x in range(2):
        for side in range(2):
            z_full[x, 0][side].wait_recv()
            add(acc.at[blocks[x][0], z], 0, rzf.at[x, side], 0, 208)
        if x == 0:
            over.append(go(acc.at[ox, z, pl.ds(0, 208)], rx.at[pl.ds(0, 208)], dx))
        z_half[x, 1][0].wait_recv()
        add(acc.at[blocks[x][0], zu], quarter(y), rzh.at[x, 0], 112, 32)
        up = go(piece(2 + x, quarter(y), 64), rzf.at[x, 0, pl.ds(208, 64)], du)
        z_half[x, 1][1].wait_recv()
        add(acc.at[blocks[x][0], zd], quarter(y) + 32, rzh.at[x, 1], 112, 32)
        z_full[x, 1] = (up, go(piece(4 + x, quarter(y), 64), rzf.at[x, 1, pl.ds(208, 64)], dd))
    for x in range(2):
        for side in range(2):
            z_full[x, 1][side].wait_recv()
            add(acc.at[blocks[x][0], z], quarter(y), rzf.at[x, side], 208, 64)
        if x == 0:
            over.append(go(acc.at[ox, z, pl.ds(208, 256)], rx.at[pl.ds(208, 256)], dx))
    own = acc.at[xl, z]
    over[0].wait_recv()
    add(own, 0, rx, 0, 208)
    over[1].wait_recv()
    add(own, 208, rx, 208, 256)

    def part(k):
        return k * 112

    def mine(at, n):
        return own.at[rows(at, n)]

    tail = pl.ds(448, 16)
    keep = load(own.at[tail], small.at[y])
    tails = [go(own.at[tail], small.at[y], d) for d in (dyu, dyd, dyo)]
    half = (
        go(mine(part(yo), 48), rfh.at[0, pl.ds(0, 48)], dyu),
        go(mine(part(yo) + 48, 64), rfh.at[1], dyd),
    )
    half[0].wait_recv()
    add(own, part(yu), rfh.at[0], 0, 48)
    full_up = go(mine(part(yu), 112), rff.at[0], dyu)
    half[1].wait_recv()
    add(own, part(yd) + 48, rfh.at[1], 0, 64)
    full_down = go(mine(part(yd), 112), rff.at[1], dyd)
    keep.wait()
    for cp in tails:
        cp.wait_recv()
    for cp in tails:
        cp.wait_send()
    total = small[0].astype(jnp.float32)
    for k in range(1, 4):
        total = total + small[k].astype(jnp.float32)
    rx[tail] = total.astype(rx.dtype)
    last = load(rx.at[tail], out.at[tail])
    full_up.wait_recv()
    add(own, part(y), rff.at[0], 0, 112)
    full_down.wait_recv()
    add(own, part(y), rff.at[1], 0, 112)
    here = rows(part(y), 112)
    stay = load(own.at[here], out.at[here])
    up = go(own.at[here], out.at[here], dyu)
    down = go(own.at[here], out.at[here], dyd)
    up.wait_recv()
    lo = rows(part(yd), 48)
    far_up = go(out.at[lo], out.at[lo], dyu)
    down.wait_recv()
    hi = rows(part(yu) + 48, 64)
    far_down = go(out.at[hi], out.at[hi], dyd)
    far_up.wait_recv()
    far_down.wait_recv()
    last.wait()
    stay.wait()
    for cp in go.all:
        if not any(cp is other for other in tails):
            cp.wait_send()


def reduce_grads(gexp, gden, cid=1):
    w = gexp.shape[-1]
    low = jnp.bfloat16
    n = 90
    return pl.pallas_call(
        reduce_kernel,
        out_shape=jax.ShapeDtypeStruct((464, w), low),
        in_specs=[pl.BlockSpec(memory_space=pl.ANY)] * 2,
        out_specs=pl.BlockSpec(memory_space=pl.ANY),
        scratch_shapes=[
            pltpu.VMEM((2, 4, 464, w), low),
            pltpu.VMEM((2, 4, 464, w), low),
            pltpu.VMEM((6, 2, 32, w), low),
            pltpu.VMEM((6, 2, 64, w), low),
            pltpu.VMEM((2, 2, 144, w), low),
            pltpu.VMEM((2, 2, 272, w), low),
            pltpu.VMEM((464, w), low),
            pltpu.VMEM((2, 64, w), low),
            pltpu.VMEM((2, 112, w), low),
            pltpu.VMEM((4, 16, w), low),
            pltpu.SemaphoreType.DMA((n,)),
            pltpu.SemaphoreType.DMA((n,)),
            pltpu.SemaphoreType.DMA((20,)),
        ],
        compiler_params=pltpu.CompilerParams(
            collective_id=cid, has_side_effects=True, vmem_limit_bytes=60 * 1024 * 1024
        ),
    )(gexp, gden)


HEADS = 12
CAPACITY = 72
LANES = 128
SLOT_ROWS = 80
TOKENS = 208
STEPS = 8
EPSILON = 1e-06
LOW = jnp.bfloat16
F32 = jnp.float32
NT = (((1,), (1,)), ((), ()))
TN = (((0,), (0,)), ((), ()))


def mm(a, b, dims=(((1,), (0,)), ((), ()))):
    return lax.dot_general(a, b, dims, preferred_element_type=F32)


def norm_parts(values):
    centre = values - jnp.mean(values, axis=-1, keepdims=True)
    rstd = lax.rsqrt(jnp.mean(centre * centre, axis=-1, keepdims=True) + EPSILON)
    return centre * rstd, rstd


def norm_back(grad, xhat, rstd, gain):
    h = grad * gain
    return rstd * (
        h - jnp.mean(h, axis=-1, keepdims=True) - xhat * jnp.mean(h * xhat, axis=-1, keepdims=True)
    )


def soft_parts(scores):
    expo = jnp.exp(scores - jnp.max(scores, axis=-1, keepdims=True))
    return expo / jnp.sum(expo, axis=-1, keepdims=True)


def route_tables(routes):
    first, second = routes[:, 0:1], routes[:, 1:2]
    lane = lax.broadcasted_iota(jnp.int32, (TOKENS, LANES), 1)
    hot_one = (lane == first).astype(F32)
    hot_two = (lane == second).astype(F32)
    earlier = (
        lax.broadcasted_iota(jnp.int32, (TOKENS, TOKENS), 1)
        < lax.broadcasted_iota(jnp.int32, (TOKENS, TOKENS), 0)
    ).astype(LOW)
    before_one = mm(earlier, hot_one.astype(LOW))
    before_two = mm(earlier, hot_two.astype(LOW)) + jnp.sum(hot_one, axis=0, keepdims=True)
    slot = lax.broadcasted_iota(jnp.int32, (TOKENS, 256), 1)

    def table(hot, before, picked):
        position = jnp.sum(before * hot, axis=1, keepdims=True).astype(jnp.int32)
        kept = (position < CAPACITY) & (picked >= 0)
        ids = jnp.where(kept, picked * SLOT_ROWS + position, 512)
        return (slot == ids).astype(F32).astype(LOW)

    return table(hot_one, before_one, first), table(hot_two, before_two, second), hot_one, hot_two


def score_mask():
    return lax.broadcasted_iota(jnp.int32, (TOKENS, TOKENS), 1) < 197


def unpack_proj(proj_ref, wp):
    for owner in range(16):
        for k in range(3):
            wp[pl.ds(owner * 48 + k * 16, 16), :] = proj_ref[owner, :, pl.ds(k * 768, 768)]


def expert_block(ref, e):
    return ref[:, :, pl.ds(e * 768, 768)].reshape(384, 768)


def slots_of(e):
    return pl.ds(e * SLOT_ROWS, SLOT_ROWS)


def tanh_part(x):
    return jnp.tanh(0.7978845608028654 * (x + 0.044715 * (x * x * x)))


def forward_kernel(
    at, inputs, received, routes, qkv, proj, router, norms, w_in, w_out, *rest
):
    (sent, section_out, c_u, c_nin, c_pro, c_mix, c_res, c_nrm, c_gate, c_slot, c_pre, c_hid, c_result,
     wp, acc, table_one, table_two) = rest[-17:]
    step = pl.program_id(0)

    @pl.when(step == 0)
    def _():
        u_low = jnp.where(at[1] == 0, inputs[0], received[...])
        c_u[0] = u_low
        u = u_low.astype(F32)
        xhat, _ = norm_parts(u)
        nin = (xhat * norms[0:1, :] + norms[2:3, :]).astype(LOW)
        c_nin[0] = nin
        for k in range(3):
            cols = pl.ds(k * 768, 768)
            c_pro[0, :, cols] = mm(nin, qkv[:, :, cols].reshape(768, 768)).astype(LOW)
        mask = score_mask()
        low_half = lax.broadcasted_iota(jnp.int32, (TOKENS, LANES), 1) < 64
        for pair in range(HEADS // 2):
            q = c_pro[0, :, pl.ds(pair * LANES, LANES)]
            k = c_pro[0, :, pl.ds(768 + pair * LANES, LANES)]
            v = c_pro[0, :, pl.ds(1536 + pair * LANES, LANES)]
            outs = []
            for half in range(2):
                qh = jnp.where(low_half if half == 0 else ~low_half, q, jnp.zeros_like(q))
                scores = jnp.where(mask, mm(qh, k, NT) * 0.125, -1e30)
                outs.append(mm(soft_parts(scores).astype(LOW), v))
            c_mix[0, :, pl.ds(pair * LANES, LANES)] = jnp.where(low_half, outs[0], outs[1]).astype(LOW)
        unpack_proj(proj, wp)
        residual = u + mm(c_mix[0], wp[...])
        c_res[0] = residual
        xhat, _ = norm_parts(residual)
        normed = (xhat * norms[1:2, :] + norms[3:4, :]).astype(LOW)
        c_nrm[0] = normed
        logits = mm(normed, router[...])
        lane = lax.broadcasted_iota(jnp.int32, (TOKENS, LANES), 1)
        c_gate[0] = soft_parts(jnp.where(lane < 3, logits, -1e30))
        one, two, _, _ = route_tables(routes[0])
        table_one[...] = one
        table_two[...] = two
        c_slot[0] = mm(one + two, normed, TN).astype(LOW)
        acc[...] = jnp.zeros_like(acc)

    for e in range(3):
        rows = slots_of(e)
        pre = mm(c_slot[0, rows, :], expert_block(w_in, e), NT)
        c_pre[0, rows, :] = pre
        hidden = (0.5 * pre * (1.0 + tanh_part(pre))).astype(LOW)
        c_hid[0, rows, :] = hidden
        acc[rows, :] += mm(hidden, expert_block(w_out, e))

    @pl.when(step == STEPS - 1)
    def _():
        result = acc[...].astype(LOW)
        c_result[0] = result
        lane = lax.broadcasted_iota(jnp.int32, (TOKENS, LANES), 1)
        gates = c_gate[0]
        gate_one = jnp.sum(jnp.where(lane == routes[0, :, 0:1], gates, 0.0), axis=1, keepdims=True)
        gate_two = jnp.sum(jnp.where(lane == routes[0, :, 1:2], gates, 0.0), axis=1, keepdims=True)
        y = c_res[0] + (mm(table_one[...], result) * gate_one + mm(table_two[...], result) * gate_two)
        y = y.astype(LOW)
        sent[...] = y
        section_out[0] = y[:197]


def whole(shape):
    return pl.BlockSpec(shape, lambda j, at: (0,) * len(shape))


def by_micro(shape):
    return pl.BlockSpec((1,) + shape[1:], lambda j, at: (at[0],) + (0,) * (len(shape) - 1))


def chunk(shape):
    return pl.BlockSpec((1, shape[1], 384), lambda j, at: (at[0], 0, j))


def fixed(shape, index):
    return pl.BlockSpec(shape, lambda j, at: index)


WEIGHT_IN = pl.BlockSpec((2, 192, 2304), lambda j, at: (j, 0, 0))
WEIGHT_OUT = pl.BlockSpec((2, 192, 2304), lambda j, at: (j, 1, 0))
QKV = fixed((16, 48, 2304), (0, 8, 0))
PROJ = fixed((16, 16, 2304), (0, 27, 0))
CACHE = [
    ((2, 197, 768), LOW),
    ((2, TOKENS, 768), LOW),
    ((2, TOKENS, 768), LOW),
    ((2, TOKENS, 2304), LOW),
    ((2, TOKENS, 768), LOW),
    ((2, TOKENS, 768), F32),
    ((2, TOKENS, 768), LOW),
    ((2, TOKENS, LANES), F32),
    ((2, 256, 768), LOW),
    ((2, 3 * SLOT_ROWS, 3072), F32),
    ((2, 3 * SLOT_ROWS, 3072), LOW),
    ((2, 256, 768), LOW),
]
BACK = [
    ((2, 197, 768), F32),
    ((2, 256, 768), LOW),
    ((2, 3 * SLOT_ROWS, 3072), LOW),
    ((2, TOKENS, 768), LOW),
    ((2, TOKENS, 2304), LOW),
    ((2, TOKENS, LANES), LOW),
    ((2, 8, 768), F32),
]


def held(shape):
    return chunk(shape) if shape[-1] == 3072 else by_micro(shape)


def call_tick(body, at, operands, specs, kept, kinds, scratch, flops):
    grown = list(operands)
    grown_specs = list(specs)
    aliases = {}
    if kept is not None:
        for n, array in enumerate(kept):
            aliases[1 + len(grown)] = 1 + n
            grown.append(array)
            grown_specs.append(pl.BlockSpec(memory_space=pl.ANY))
    return pl.pallas_call(
        body,
        out_shape=[jax.ShapeDtypeStruct((TOKENS, 768), LOW)]
        + [jax.ShapeDtypeStruct(shape, kind) for shape, kind in kinds],
        grid_spec=pltpu.PrefetchScalarGridSpec(
            num_scalar_prefetch=1,
            grid=(STEPS,),
            in_specs=grown_specs,
            out_specs=[whole((TOKENS, 768))] + [held(shape) for shape, _ in kinds],
            scratch_shapes=scratch,
        ),
        input_output_aliases=aliases,
        compiler_params=pltpu.CompilerParams(vmem_limit_bytes=60 * 1024 * 1024),
        cost_estimate=pl.CostEstimate(flops=flops, bytes_accessed=40_000_000, transcendentals=1_000_000),
    )(at, *grown)


def forward_tick(at, inputs, received, routes, every, router, norms, kept):
    outs = call_tick(
        forward_kernel,
        at,
        [inputs, received, routes, every, every, router, norms, every, every],
        [
            by_micro(inputs.shape), whole((TOKENS, 768)), by_micro(routes.shape), QKV, PROJ,
            whole(router.shape), whole(norms.shape), WEIGHT_IN, WEIGHT_OUT,
        ],
        kept,
        CACHE,
        [
            pltpu.VMEM((768, 768), LOW),
            pltpu.VMEM((256, 768), F32),
            pltpu.VMEM((TOKENS, 256), LOW),
            pltpu.VMEM((TOKENS, 256), LOW),
        ],
        4_000_000_000,
    )
    return outs[0], outs[1:]


def backward_kernel(
    at, cotangent, returned, routes, qkv, proj, router, norms, w_in, w_out,
    c_u, c_pro, c_res, c_gate, c_pre, c_result, *rest
):
    (sent, section_in_grad, b_gres, b_gpre, b_ga, b_gp, b_gl, b_norm,
     wp, acc, table, grad_normed_part) = rest[-12:]
    step = pl.program_id(0)

    def grad_y():
        return jnp.where(at[1] == 1, cotangent[0], returned[...]).astype(F32)

    @pl.when(step == 0)
    def _():
        gy = grad_y()
        one, two, hot_one, hot_two = route_tables(routes[0])
        table[...] = one + two
        gates = c_gate[0]
        gate_one = jnp.sum(gates * hot_one, axis=1, keepdims=True)
        gate_two = jnp.sum(gates * hot_two, axis=1, keepdims=True)
        b_gres[0] = (
            mm(one, (gy * gate_one).astype(LOW), TN) + mm(two, (gy * gate_two).astype(LOW), TN)
        ).astype(LOW)
        result = c_result[0]
        pick_one = jnp.sum(gy * mm(one, result), axis=1, keepdims=True)
        pick_two = jnp.sum(gy * mm(two, result), axis=1, keepdims=True)
        grad_gates = hot_one * pick_one + hot_two * pick_two
        grad_logits = (
            gates * (grad_gates - jnp.sum(grad_gates * gates, axis=1, keepdims=True))
        ).astype(LOW)
        b_gl[0] = grad_logits
        grad_normed_part[...] = mm(grad_logits, router[...], NT)
        acc[...] = jnp.zeros_like(acc)

    for e in range(3):
        rows = slots_of(e)
        grad_hidden = mm(b_gres[0, rows, :], expert_block(w_out, e), NT)
        x = c_pre[0, rows, :]
        t = tanh_part(x)
        slope = 0.5 * (1.0 + t) + 0.5 * x * (1.0 - t * t) * (
            0.7978845608028654 * (1.0 + 3 * 0.044715 * (x * x))
        )
        grad_pre = (slope * grad_hidden).astype(LOW)
        b_gpre[0, rows, :] = grad_pre
        acc[rows, :] += mm(grad_pre, expert_block(w_in, e))

    @pl.when(step == STEPS - 1)
    def _():
        grad_normed = mm(table[...], acc[...].astype(LOW)) + grad_normed_part[...]
        xhat, rstd = norm_parts(c_res[0])
        b_norm[0, 1:2, :] = jnp.sum(grad_normed * xhat, axis=0, keepdims=True)
        b_norm[0, 3:4, :] = jnp.sum(grad_normed, axis=0, keepdims=True)
        b_norm[0, 4:8, :] = jnp.zeros((4, 768), F32)
        grad_residual = grad_y() + norm_back(grad_normed, xhat, rstd, norms[1:2, :])
        ga = grad_residual.astype(LOW)
        b_ga[0] = ga
        unpack_proj(proj, wp)
        grad_mixed = mm(ga, wp[...], NT).astype(LOW)
        mask = score_mask()
        low_half = lax.broadcasted_iota(jnp.int32, (TOKENS, LANES), 1) < 64
        for pair in range(HEADS // 2):
            q = c_pro[0, :, pl.ds(pair * LANES, LANES)]
            k = c_pro[0, :, pl.ds(768 + pair * LANES, LANES)]
            v = c_pro[0, :, pl.ds(1536 + pair * LANES, LANES)]
            gm = grad_mixed[:, pair * LANES:(pair + 1) * LANES]
            gq, gk, gv = [], [], []
            for half in range(2):
                keep = low_half if half == 0 else ~low_half
                qh = jnp.where(keep, q, jnp.zeros_like(q))
                gh = jnp.where(keep, gm, jnp.zeros_like(gm))
                probs = soft_parts(jnp.where(mask, mm(qh, k, NT) * 0.125, -1e30))
                grad_probs = mm(gh, v, NT)
                gs = (
                    probs * (grad_probs - jnp.sum(grad_probs * probs, axis=-1, keepdims=True))
                ).astype(LOW)
                gq.append(mm(gs, k))
                gk.append(mm(gs, q, TN))
                gv.append(mm(probs.astype(LOW), gm, TN))
            b_gp[0, :, pl.ds(pair * LANES, LANES)] = (jnp.where(low_half, gq[0], gq[1]) * 0.125).astype(LOW)
            b_gp[0, :, pl.ds(768 + pair * LANES, LANES)] = (jnp.where(low_half, gk[0], gk[1]) * 0.125).astype(LOW)
            b_gp[0, :, pl.ds(1536 + pair * LANES, LANES)] = jnp.where(low_half, gv[0], gv[1]).astype(LOW)
        grad_nin = jnp.zeros((TOKENS, 768), F32)
        for k in range(3):
            cols = pl.ds(k * 768, 768)
            grad_nin = grad_nin + mm(b_gp[0, :, cols], qkv[:, :, cols].reshape(768, 768), NT)
        xhat, rstd = norm_parts(c_u[0].astype(F32))
        b_norm[0, 0:1, :] = jnp.sum(grad_nin * xhat, axis=0, keepdims=True)
        b_norm[0, 2:3, :] = jnp.sum(grad_nin, axis=0, keepdims=True)
        grad_in = grad_residual + norm_back(grad_nin, xhat, rstd, norms[0:1, :])
        section_in_grad[0] = grad_in[:197]
        sent[...] = grad_in.astype(LOW)


def backward_tick(at, cotangent, returned, routes, every, router, norms, caches, kept):
    _, c_u, _, c_pro, _, c_res, _, c_gate, _, c_pre, _, c_result = caches
    mine = [c_u, c_pro, c_res, c_gate, c_pre, c_result]
    outs = call_tick(
        backward_kernel,
        at,
        [cotangent, returned, routes, every, every, router, norms, every, every] + mine,
        [
            by_micro(cotangent.shape), whole((TOKENS, 768)), by_micro(routes.shape), QKV, PROJ,
            whole(router.shape), whole(norms.shape), WEIGHT_IN, WEIGHT_OUT,
        ]
        + [held(array.shape) for array in mine],
        kept,
        BACK,
        [
            pltpu.VMEM((768, 768), LOW),
            pltpu.VMEM((256, 768), F32),
            pltpu.VMEM((TOKENS, 256), LOW),
            pltpu.VMEM((TOKENS, 768), F32),
        ],
        6_000_000_000,
    )
    return outs[0], outs[1:]


def weight_kernel(c_nin, c_mix, c_nrm, c_slot, c_hid, b_gres, b_gpre, b_ga, b_gp, b_gl, b_norm, gexp, gden):
    step = pl.program_id(0)

    def both(ref, rows=None):
        if rows is None:
            return jnp.concatenate([ref[0], ref[1]], axis=0)
        return jnp.concatenate([ref[0, rows, :], ref[1, rows, :]], axis=0)

    for e in range(3):
        rows = slots_of(e)
        cols = pl.ds(e * 768, 768)
        first = mm(both(b_gpre, rows), both(c_slot, rows), TN).astype(LOW)
        second = mm(both(c_hid, rows), both(b_gres, rows), TN).astype(LOW)
        for owner in range(2):
            gexp[owner, pl.ds(0, 192), cols] = first[owner * 192:(owner + 1) * 192]
            gexp[owner, pl.ds(192, 192), cols] = second[owner * 192:(owner + 1) * 192]

    for k in range(3):
        @pl.when(step == k)
        def _(k=k):
            cols = pl.ds(k * 768, 768)
            grad = mm(both(c_nin), jnp.concatenate([b_gp[0, :, cols], b_gp[1, :, cols]], axis=0), TN).astype(LOW)
            for owner in range(16):
                gden[owner, pl.ds(0, 48), cols] = grad[owner * 48:(owner + 1) * 48]

    @pl.when(step == 3)
    def _():
        grad = mm(both(c_mix), both(b_ga), TN).astype(LOW)
        for owner in range(16):
            for k in range(3):
                at = owner * 48 + k * 16
                gden[owner, pl.ds(48, 16), pl.ds(k * 768, 768)] = grad[at:at + 16]

    @pl.when(step == 4)
    def _():
        router = mm(both(b_gl), both(c_nrm), TN)[:8]
        small = jnp.concatenate([router, b_norm[0] + b_norm[1]], axis=0).astype(LOW)
        for owner in range(16):
            gden[owner, pl.ds(64, 16), pl.ds(0, 768)] = small
            gden[owner, pl.ds(64, 16), pl.ds(768, 1536)] = jnp.zeros((16, 1536), LOW)


def weight_grads(caches, backs):
    _, _, c_nin, _, c_mix, _, c_nrm, _, c_slot, _, c_hid, _ = caches
    _, b_gres, b_gpre, b_ga, b_gp, b_gl, b_norm = backs
    operands = [c_nin, c_mix, c_nrm, c_slot, c_hid, b_gres, b_gpre, b_ga, b_gp, b_gl, b_norm]

    def spec(shape):
        if shape[-1] == 3072:
            return pl.BlockSpec((2, shape[1], 384), lambda j: (0, 0, j))
        return pl.BlockSpec(shape, lambda j: (0, 0, 0))

    return pl.pallas_call(
        weight_kernel,
        out_shape=[
            jax.ShapeDtypeStruct((16, 384, 2304), LOW),
            jax.ShapeDtypeStruct((16, 80, 2304), LOW),
        ],
        grid=(STEPS,),
        in_specs=[spec(array.shape) for array in operands],
        out_specs=[
            pl.BlockSpec((2, 384, 2304), lambda j: (j, 0, 0)),
            pl.BlockSpec((16, 80, 2304), lambda j: (0, 0, 0)),
        ],
        compiler_params=pltpu.CompilerParams(vmem_limit_bytes=60 * 1024 * 1024),
    )(*operands)


def to_section(value, by):
    pairs = [(i, i + by) for i in range(2) if 0 <= i + by < 2]
    return lax.ppermute(value, "section", pairs)


def local(
    inputs, cotangent, routes, norm_gain, norm_offset, w_qkv, w_proj, w_router, experts_in, experts_out
):
    section = lax.axis_index("section")
    small = jnp.concatenate([w_router[0], norm_gain[0].T, norm_offset[0].T], axis=1)
    own = jnp.concatenate(
        [
            experts_in[0].reshape(192, 2304),
            experts_out[0].reshape(192, 2304),
            w_qkv[0],
            w_proj[0].reshape(3, 16, 768).transpose(1, 0, 2).reshape(16, 2304),
            jnp.pad(small.reshape(16, 21), ((0, 0), (0, 2283))),
        ],
        axis=0,
    )
    every = gather(own, 208).reshape(16, 464, 2304)
    small = every[:, 448:, :21].reshape(768, 7)
    router = jnp.pad(small[:, :3], ((0, 0), (0, LANES - 3)))
    norms = jnp.pad(small[:, 3:].T.astype(F32), ((0, 4), (0, 0)))
    pad = ((0, 0), (0, TOKENS - 197), (0, 0))
    inputs = jnp.pad(inputs[:, 0], pad)
    cotangent = jnp.pad(cotangent[:, 0], pad)
    routes = jnp.pad(routes[0, :, 0], ((0, 0), (0, TOKENS - 197), (0, LANES - 2)), constant_values=-1)
    received = jnp.zeros((TOKENS, 768), LOW)
    caches = None
    for tick in range(3):
        at = jnp.stack([jnp.clip(tick - section, 0, 1), section]).astype(jnp.int32)
        sent, caches = forward_tick(at, inputs, received, routes, every, router, norms, caches)
        if tick < 2:
            received = to_section(sent, 1)
    returned = jnp.zeros((TOKENS, 768), LOW)
    backs = None
    for tick in range(3):
        at = jnp.stack([jnp.clip(tick - 1 + section, 0, 1), section]).astype(jnp.int32)
        sent, backs = backward_tick(at, cotangent, returned, routes, every, router, norms, caches, backs)
        if tick < 2:
            returned = to_section(sent, -1)
    gexp, gden = weight_grads(caches, backs)
    total = reduce_grads(gexp.reshape(2, 4, 2, 384, 2304), gden.reshape(2, 4, 2, 80, 2304)).astype(F32)
    mine = lax.dynamic_slice_in_dim(total[448:, :768], lax.axis_index("shard") * 48, 48, axis=1)
    return (
        caches[0][None, :, None],
        backs[0][None, :, None],
        mine[8:10][None],
        mine[10:12][None],
        total[384:432][None],
        total[432:448].reshape(16, 3, 768).transpose(1, 0, 2).reshape(1, 48, 768),
        mine[:3].T[None],
        total[:192].reshape(1, 192, 3, 768),
        total[192:384].reshape(1, 192, 3, 768),
    )


def solution(mesh):
    return jax.shard_map(
        local,
        mesh=mesh,
        in_specs=(
            P(None, ("replica", "shard"), None, None),
            P(None, ("replica", "shard"), None, None),
            P("section", None, ("replica", "shard"), None, None),
            P("section", None, "shard"),
            P("section", None, "shard"),
            P("section", "shard", None),
            P("section", "shard", None),
            P("section", "shard", None),
            P("section", "shard", None, None),
            P("section", "shard", None, None),
        ),
        out_specs=(
            P("section", None, ("replica", "shard"), None, None),
            P("section", None, ("replica", "shard"), None, None),
            P("section", None, "shard"),
            P("section", None, "shard"),
            P("section", "shard", None),
            P("section", "shard", None),
            P("section", "shard", None),
            P("section", "shard", None, None),
            P("section", "shard", None, None),
        ),
        check_vma=False,
    )
```

time: 1080 us -> 544 us (0.50)
  waiting for transfers between devices: 564 us -> 26.6 us
  Pallas kernels: 0 us -> 451 us
  matrix products: 210 us -> 0 us
  local copies, waits for them, and re-layouts: 117 us -> 37.2 us
  other arithmetic: 78.7 us -> 6.42 us
  blocking collectives: 69.7 us -> 0 us
  between operations: 16.7 us -> 1.44 us
    pallas_call x0 -> x9, Pallas kernels: none -> 451 us  [the longest x6 171 us: call_tick(): pl.pallas_call(body, out_shape=[jax.ShapeDtypeStruct((TOKENS, 768), LOW)]...]
    dot_general x71 -> x0, matrix products: 210 us -> none  [the longest x3 31 us: expert_backward(): jnp.einsum('ced,red->cer', grad_slots, piece_out, preferred_element_type=...]
    reduce_scatter x3 -> x0, waiting for transfers between devices: 192 us -> none  [the longest x1 160 us: local(): lax.psum_scatter(jnp.stack([grad_first, grad_second], axis=1).astype(jnp....]
    unnamed x14 -> x0, waiting for transfers between devices: 176 us -> none
    all_gather x4 -> x0, waiting for transfers between devices: 132 us -> none  [the longest x1 72.3 us: expert_forward(): piece_out = lax.all_gather(experts_out, 'shard', axis=0, tiled=True)]
    all_gather x3 -> x0, blocking collectives: 61.1 us -> none  [the longest x1 24 us: local(): lax.all_gather(norm_offset[0], 'shard', axis=1, tiled=True)]
    psum x1 -> x0, waiting for transfers between devices: 52.5 us -> none  [local(): lax.psum(shard_qkv.astype(jnp.bfloat16), 'replica').astype(jnp.float32)]
    another operation x35 -> x6, other arithmetic: 43.8 us -> 3.51 us  [the longest x3 1.76 us: local(): jnp.stack([jnp.clip(tick - 1 + section, 0, 1), section]).astype(jnp.int32)]
  transfers between devices with their start and end apart: 15 -> 4, of which waited for: 11 -> 4; matrix products, arithmetic and copies ran while one was open for 16% -> 1% of each run, Pallas kernels for 0% -> 0%
where the time goes in v1:
time: 544 us; the launch traced here: 536 us
  Pallas kernels  451 us (83%)
  local copies, waits for them, and re-layouts  37.2 us (7%)
  waiting for transfers between devices  26.6 us (5%)
  starting transfers between devices  13 us (2%)
  other arithmetic  6.42 us (1%)
    pallas_call x6, Pallas kernels, call_tick(): pl.pallas_call(body, out_shape=[jax.ShapeDtypeStruct((TOKENS, 768), LOW)]...  171 us
    pallas_call x1, Pallas kernels, reduce_grads(): pl.pallas_call(reduce_kernel, out_shape=jax.ShapeDtypeStruct((464, w), lo...  162 us
    pallas_call x1, Pallas kernels, gather(): pl.pallas_call(body, out_shape=jax.ShapeDtypeStruct((2, 4, 2, r, w), own....  97.2 us
    ppermute x4, waiting for transfers between devices, to_section(): return lax.ppermute(value, 'section', pairs)  26.6 us
    pallas_call x1, Pallas kernels, weight_grads(): pl.pallas_call(weight_kernel, out_shape=[jax.ShapeDtypeStruct((16, 384, 2...  21 us
    unnamed x52, local copies, waits for them, and re-layouts  18 us
    ppermute x4, starting transfers between devices, to_section(): return lax.ppermute(value, 'section', pairs)  13 us
  transfers between devices with their start and end apart: 4, of which 4 were waited for; matrix products, arithmetic and copies ran while one was open for 1% of the time, Pallas kernels for 0%

profile of v1, /device:TPU:1, one launch (start us, length us, event | category | flops | bytes accessed | tf_op | source)
XLA Modules:
  0.0 536.0 jit_solution(1980852676497435212)
XLA Ops:
  0.6 1.9 copy.86
  6.9 97.2 %shard_map.169 = bf16[2,4,2,464,2304]{4,3,2,1,0:T(8,128)(2,1)} custom-call(bf16[464,2304]{1,0:T(8,128)(2,1)} %copy-done.3), custom_call_target="tpu_custom_call" | custom-call | tf_op jit(solution)/shard_map/pallas_call | solution.py:150
  109.8 25.8 %shard_map.170 = (bf16[208,768]{1,0:T(8,128)(2,1)}, bf16[2,197,768]{2,1,0:T(8,128)(2,1)}, bf16[2,208,768]{2,1,0:T(8,128)(2,1)}, bf16[2,208,768]{2,1,0:T(8,128)(2...) custom-call(s32[2]{0:T(128)} %pad_add_fusion.2.at, ...), custom_call_target="tpu_custom_call" | custom-call | flops 4000000000 | bytes 40000000 | tf_op jit(solution)/shard_map/pallas_call | solution.py:565
  135.7 4.9 collective-permute-start
  141.2 6.4 %collective-permute-done.received = bf16[208,768]{1,0:T(8,128)(2,1)S(1)} collective-permute-done((bf16[208,768]{1,0:T(8,128)(2,1)}, bf16[208,768]{1,0:T(8,128)(2,1)S(1)}, u32[]{:S(2)}, u32[]{:S(2)}) %collective-permute-start) | collective-permute-done | bytes 319520 | tf_op jit(solution)/shard_map/ppermute | solution.py:791
  148.3 26.0 %shard_map.171 = (bf16[208,768]{1,0:T(8,128)(2,1)}, bf16[2,197,768]{2,1,0:T(8,128)(2,1)}, bf16[2,208,768]{2,1,0:T(8,128)(2,1)}, bf16[2,208,768]{2,1,0:T(8,128)(2...) custom-call(s32[2]{0:T(128)} %pad_add_fusion.1.at, ...), custom_call_target="tpu_custom_call", output_to_operand_aliasing={{1}: (10, {}), {2}: (11, {}), {3}: (12, {}), {4}: (13, {}),... | custom-call | flops 4000000000 | bytes 40000000 | tf_op jit(solution)/shard_map/pallas_call | solution.py:565
  174.3 5.5 %collective-permute-start.1 = (bf16[208,768]{1,0:T(8,128)(2,1)}, bf16[208,768]{1,0:T(8,128)(2,1)S(1)}, u32[]{:S(2)}, u32[]{:S(2)}) collective-permute-start(bf16[208,768]{1,0:T(8,128)(2,1)} %get-tuple-element.85), channel_id=1, source_target_pairs={{0,64},{1,65},{2,66},{3,67},{4,68},{5,69},{6,70},{7,71},{8,72},{9,... | collective-permute-start | bytes 958472 | tf_op jit(solution)/shard_map/ppermute | solution.py:791
  182.0 4.2 collective-permute-done.1.received
  186.9 25.8 %shard_map.172 = (bf16[208,768]{1,0:T(8,128)(2,1)}, bf16[2,197,768]{2,1,0:T(8,128)(2,1)}, bf16[2,208,768]{2,1,0:T(8,128)(2,1)}, bf16[2,208,768]{2,1,0:T(8,128)(2...) custom-call(s32[2]{0:T(128)} %pad_add_fusion.at, ...), custom_call_target="tpu_custom_call", output_to_operand_aliasing={{1}: (10, {}), {2}: (11, {}), {3}: (12, {}), {4}: (13, {}),... | custom-call | flops 4000000000 | bytes 40000000 | tf_op jit(solution)/shard_map/pallas_call | solution.py:565
  212.7 31.4 %shard_map.173 = (bf16[208,768]{1,0:T(8,128)(2,1)}, f32[2,197,768]{2,1,0:T(8,128)}, bf16[2,256,768]{2,1,0:T(8,128)(2,1)}, bf16[2,240,3072]{2,1,0:T(8,128)(2,1)},...) custom-call(s32[2]{0:T(128)} %pad_add_fusion.5.at, ...), custom_call_target="tpu_custom_call" | custom-call | flops 6000000000 | bytes 40000000 | tf_op jit(solution)/shard_map/pallas_call | solution.py:565
  246.0 9.1 %collective-permute-done.2.returned = bf16[208,768]{1,0:T(8,128)(2,1)S(1)} collective-permute-done((bf16[208,768]{1,0:T(8,128)(2,1)}, bf16[208,768]{1,0:T(8,128)(2,1)S(1)}, u32[]{:S(2)}, u32[]{:S(2)}) %collective-permute-start.2) | collective-permute-done | bytes 319520 | tf_op jit(solution)/shard_map/ppermute | solution.py:791
  255.8 31.2 %shard_map.174 = (bf16[208,768]{1,0:T(8,128)(2,1)}, f32[2,197,768]{2,1,0:T(8,128)}, bf16[2,256,768]{2,1,0:T(8,128)(2,1)}, bf16[2,240,3072]{2,1,0:T(8,128)(2,1)},...) custom-call(s32[2]{0:T(128)} %pad_add_fusion.4.at, ...), custom_call_target="tpu_custom_call", output_to_operand_aliasing={{1}: (16, {}), {2}: (17, {}), {3}: (18, {}), {4}: (19, {}),... | custom-call | flops 6000000000 | bytes 40000000 | tf_op jit(solution)/shard_map/pallas_call | solution.py:565
  290.2 6.9 %collective-permute-done.3.returned = bf16[208,768]{1,0:T(8,128)(2,1)S(1)} collective-permute-done((bf16[208,768]{1,0:T(8,128)(2,1)}, bf16[208,768]{1,0:T(8,128)(2,1)S(1)}, u32[]{:S(2)}, u32[]{:S(2)}) %collective-permute-start.3) | collective-permute-done | bytes 319520 | tf_op jit(solution)/shard_map/ppermute | solution.py:791
  297.8 31.1 %shard_map.175 = (bf16[208,768]{1,0:T(8,128)(2,1)}, f32[2,197,768]{2,1,0:T(8,128)}, bf16[2,256,768]{2,1,0:T(8,128)(2,1)}, bf16[2,240,3072]{2,1,0:T(8,128)(2,1)},...) custom-call(s32[2]{0:T(128)} %pad_add_fusion.3.at, ...), custom_call_target="tpu_custom_call", output_to_operand_aliasing={{1}: (16, {}), {2}: (17, {}), {3}: (18, {}), {4}: (19, {}),... | custom-call | flops 6000000000 | bytes 40000000 | tf_op jit(solution)/shard_map/pallas_call | solution.py:565
  328.9 21.0 %shard_map.176 = (bf16[16,384,2304]{2,1,0:T(8,128)(2,1)}, bf16[16,80,2304]{2,1,0:T(8,128)(2,1)}) custom-call(bf16[2,208,768]{2,1,0:T(8,128)(2,1)} %get-tuple-element.122.c_nin, bf16[2,208,768]{2,1,0:T(8,128)(2,1)} %get-tuple-element.123.c_mix, bf16[2,208,768]{2,1,0:T(8,128)(2,1)} %get-tuple-element.124.c_nrm, ...), custom_call_target="tpu_custom_call" | custom-call | tf_op jit(solution)/shard_map/pallas_call | solution.py:773
  349.9 161.9 %shard_map.177 = bf16[464,2304]{1,0:T(8,128)(2,1)} custom-call(bf16[2,4,2,384,2304]{4,3,2,1,0:T(8,128)(2,1)} %bitcast.77, bf16[2,4,2,80,2304]{4,3,2,1,0:T(8,128)(2,1)} %bitcast.79), custom_call_target="tpu_custom_call" | custom-call | tf_op jit(solution)/shard_map/pallas_call | solution.py:335
  511.8 3.6 fusion
  515.4 2.3 convert_element_type.17
  517.7 2.8 reshape.56
  520.5 1.5 copy.96
  522.0 4.1 reshape.57
  526.1 3.3 copy.97
  529.4 1.8 slice_bitcast_fusion
  532.6 2.3 copy.94
  (76 shorter events, 22.6 us)
Async XLA Ops:
  2.6 1.2 copy-start.4
  3.8 0.9 copy-start.12
  3.8 1.0 copy-start.14
  3.8 1.0 copy-start.15
  3.8 1.0 copy-start.16
  4.5 0.9 copy-start.11
  5.5 1.3 copy-start.3
  6.8 99.1 %copy-start.13 = (s32[1,2,1,197,2]{3,4,2,1,0:T(2,128)S(1)}, s32[1,2,1,197,2]{3,4,2,1,0:T(2,128)}, u32[]{:S(2)}) copy-start(s32[1,2,1,197,2]{3,4,2,1,0:T(2,128)} %param.12) | copy-start | bytes 9460
  6.8 99.2 %copy-start.5 = (bf16[2,1,197,768]{3,0,2,1:T(2,128)(2,1)S(1)}, bf16[2,1,197,768]{3,0,2,1:T(2,128)(2,1)}, u32[]{:S(2)}) copy-start(bf16[2,1,197,768]{3,0,2,1:T(2,128)(2,1)} %param.10) | copy-start | bytes 1815556
  135.7 11.9 %collective-permute-start = (bf16[208,768]{1,0:T(8,128)(2,1)}, bf16[208,768]{1,0:T(8,128)(2,1)S(1)}, u32[]{:S(2)}, u32[]{:S(2)}) collective-permute-start(bf16[208,768]{1,0:T(8,128)(2,1)} %get-tuple-element.72), channel_id=1, source_target_pairs={{0,64},{1,65},{2,66},{3,67},{4,68},{5,69},{6,70},{7,71},{8,72},{9,... | collective-permute-start | bytes 958472 | tf_op jit(solution)/shard_map/ppermute | solution.py:791
  147.6 0.7 copy-start.8
  148.3 31.5 %copy-start.6 = (bf16[2,1,197,768]{3,0,2,1:T(2,128)(2,1)S(1)}, bf16[2,1,197,768]{3,0,2,1:T(2,128)(2,1)}, u32[]{:S(2)}) copy-start(bf16[2,1,197,768]{3,0,2,1:T(2,128)(2,1)} %param.11) | copy-start | bytes 1815556
  174.3 11.9 %collective-permute-start.1 = (bf16[208,768]{1,0:T(8,128)(2,1)}, bf16[208,768]{1,0:T(8,128)(2,1)S(1)}, u32[]{:S(2)}, u32[]{:S(2)}) collective-permute-start(bf16[208,768]{1,0:T(8,128)(2,1)} %get-tuple-element.85), channel_id=1, source_target_pairs={{0,64},{1,65},{2,66},{3,67},{4,68},{5,69},{6,70},{7,71},{8,72},{9,... | collective-permute-start | bytes 958472 | tf_op jit(solution)/shard_map/ppermute | solution.py:791
  186.2 0.7 copy-start.7
  244.1 11.0 %collective-permute-start.2 = (bf16[208,768]{1,0:T(8,128)(2,1)}, bf16[208,768]{1,0:T(8,128)(2,1)S(1)}, u32[]{:S(2)}, u32[]{:S(2)}) collective-permute-start(bf16[208,768]{1,0:T(8,128)(2,1)} %get-tuple-element.105), channel_id=1, source_target_pairs={{64,0},{65,1},{66,2},{67,3},{68,4},{69,5},{70,6},{71,7},{72,8},{73... | collective-permute-start | bytes 958472 | tf_op jit(solution)/shard_map/ppermute | solution.py:791
  255.1 0.7 copy-start.10
  255.8 33.1 %copy-start.2 = (bf16[2,197,768]{2,1,0:T(8,128)(2,1)S(1)}, bf16[2,197,768]{2,1,0:T(8,128)(2,1)}, u32[]{:S(2)}) copy-start(bf16[2,197,768]{2,1,0:T(8,128)(2,1)} %get-tuple-element.98) | copy-start | bytes 1815556
  287.0 10.0 %collective-permute-start.3 = (bf16[208,768]{1,0:T(8,128)(2,1)}, bf16[208,768]{1,0:T(8,128)(2,1)S(1)}, u32[]{:S(2)}, u32[]{:S(2)}) collective-permute-start(bf16[208,768]{1,0:T(8,128)(2,1)} %get-tuple-element.113), channel_id=1, source_target_pairs={{64,0},{65,1},{66,2},{67,3},{68,4},{69,5},{70,6},{71,7},{72,8},{73... | collective-permute-start | bytes 958472 | tf_op jit(solution)/shard_map/ppermute | solution.py:791
  297.1 0.7 copy-start.9
  511.8 3.6 copy-start
  526.1 6.5 %copy-start.1 = (f32[2,197,768]{2,1,0:T(8,128)S(1)}, f32[2,197,768]{2,1,0:T(8,128)}, u32[]{:S(2)}) copy-start(f32[2,197,768]{2,1,0:T(8,128)} %get-tuple-element.121) | copy-start | bytes 3631108

commit v2 on v1

--- a/solution.py
+++ b/solution.py
@@ -157,7 +157,7 @@
     )(own)
 
 
-def reduce_kernel(gexp, gden, out, acc, rc, ryh, ryf, rzh, rzf, rx, rfh, rff, small, send, recv, loc):
+def reduce_kernel(gexp, gden, out, acc, rc, ryh, ryf, rzh, rzf, rx, rfh, rff, tfh, tff, small, send, recv, loc):
     xl, z, c, y = place()
     ox, zu, zd, zo = 1 - xl, (z + 1) % 4, (z + 3) % 4, (z + 2) % 4
     yu, yd, yo = (y + 1) % 4, (y + 3) % 4, (y + 2) % 4
@@ -182,7 +182,7 @@
         lax.fori_loop(0, n // 16, body, 0)
 
     blocks = [(ox, zo), (xl, zo), (ox, zu), (xl, zu), (ox, zd), (xl, zd), (ox, z), (xl, z)]
-    exp_rows, den_rows = pl.ds(0, 384), pl.ds(384, 80)
+    exp_rows, den_rows = pl.ds(80, 384), pl.ds(0, 80)
     parts = []
     for a, b in blocks:
         parts.append((
@@ -240,6 +240,7 @@
                 add(acc.at[blocks[x][0], zd], 96, rzh.at[x, 1], 0, 112)
                 z_full[x, 0] = (up, go(piece(4 + x, 0, 208), rzf.at[x, 1, pl.ds(0, 208)], dd))
     own_sum(6)
+    early = [go(acc.at[ox, z, rows(quarter(k), 64)], rx.at[rows(quarter(k), 64)], dx) for k in (yu, yd, yo)]
     own_sum(7)
     for t in range(6):
         a, b = blocks[t]
@@ -251,6 +252,51 @@
                 go(piece(t, quarter(y), 32), rzh.at[t, 0, pl.ds(112, 32)], du),
                 go(piece(t, quarter(y) + 32, 32), rzh.at[t, 1, pl.ds(112, 32)], dd),
             )
+    own = acc.at[xl, z]
+    for cp, k in zip(early, (yu, yd, yo)):
+        cp.wait_recv()
+        add(own, quarter(k), rx, quarter(k), 64)
+
+    def mine(at, n):
+        return own.at[rows(at, n)]
+
+    def finish(base, q, halfway, whole_part):
+        low, high = halves(q)
+
+        def part(k):
+            return base + k * q
+
+        half_up = go(mine(part(yo), low), halfway.at[0, pl.ds(0, low)], dyu)
+        half_down = go(mine(part(yo) + low, high), halfway.at[1, pl.ds(0, high)], dyd)
+        yield
+        half_up.wait_recv()
+        add(own, part(yu), halfway.at[0], 0, low)
+        full_up = go(mine(part(yu), q), whole_part.at[0], dyu)
+        half_down.wait_recv()
+        add(own, part(yd) + low, halfway.at[1], 0, high)
+        full_down = go(mine(part(yd), q), whole_part.at[1], dyd)
+        yield
+        full_up.wait_recv()
+        add(own, part(y), whole_part.at[0], 0, q)
+        full_down.wait_recv()
+        add(own, part(y), whole_part.at[1], 0, q)
+        here = rows(part(y), q)
+        up = go(own.at[here], out.at[here], dyu)
+        down = go(own.at[here], out.at[here], dyd)
+        stay = load(own.at[here], out.at[here])
+        yield
+        up.wait_recv()
+        lo = rows(part(yd), low)
+        far_up = go(out.at[lo], out.at[lo], dyu)
+        down.wait_recv()
+        hi = rows(part(yu) + low, high)
+        far_down = go(out.at[hi], out.at[hi], dyd)
+        yield
+        far_up.wait_recv()
+        far_down.wait_recv()
+        stay.wait()
+        yield
+
     over = []
     for x in range(2):
         for side in range(2):
@@ -264,37 +310,26 @@
         z_half[x, 1][1].wait_recv()
         add(acc.at[blocks[x][0], zd], quarter(y) + 32, rzh.at[x, 1], 112, 32)
         z_full[x, 1] = (up, go(piece(4 + x, quarter(y), 64), rzf.at[x, 1, pl.ds(208, 64)], dd))
+    tail = pl.ds(0, 16)
+    end_one = finish(16, 48, tfh, tff)
+    end_two = finish(208, 64, rfh, rff)
     for x in range(2):
         for side in range(2):
             z_full[x, 1][side].wait_recv()
             add(acc.at[blocks[x][0], z], quarter(y), rzf.at[x, side], 208, 64)
         if x == 0:
-            over.append(go(acc.at[ox, z, pl.ds(208, 256)], rx.at[pl.ds(208, 256)], dx))
-    own = acc.at[xl, z]
-    over[0].wait_recv()
-    add(own, 0, rx, 0, 208)
+            over.append(go(acc.at[ox, z, rows(quarter(y), 64)], rx.at[rows(quarter(y), 64)], dx))
+            over[0].wait_recv()
+            add(own, 0, rx, 0, 208)
+            keep = load(own.at[tail], small.at[y])
+            tails = [go(own.at[tail], small.at[y], d) for d in (dyu, dyd, dyo)]
+            next(end_one)
     over[1].wait_recv()
-    add(own, 208, rx, 208, 256)
-
-    def part(k):
-        return k * 112
-
-    def mine(at, n):
-        return own.at[rows(at, n)]
-
-    tail = pl.ds(448, 16)
-    keep = load(own.at[tail], small.at[y])
-    tails = [go(own.at[tail], small.at[y], d) for d in (dyu, dyd, dyo)]
-    half = (
-        go(mine(part(yo), 48), rfh.at[0, pl.ds(0, 48)], dyu),
-        go(mine(part(yo) + 48, 64), rfh.at[1], dyd),
-    )
-    half[0].wait_recv()
-    add(own, part(yu), rfh.at[0], 0, 48)
-    full_up = go(mine(part(yu), 112), rff.at[0], dyu)
-    half[1].wait_recv()
-    add(own, part(yd) + 48, rfh.at[1], 0, 64)
-    full_down = go(mine(part(yd), 112), rff.at[1], dyd)
+    add(own, quarter(y), rx, quarter(y), 64)
+    next(end_two)
+    next(end_one)
+    next(end_two)
+    next(end_one)
     keep.wait()
     for cp in tails:
         cp.wait_recv()
@@ -305,24 +340,12 @@
         total = total + small[k].astype(jnp.float32)
     rx[tail] = total.astype(rx.dtype)
     last = load(rx.at[tail], out.at[tail])
-    full_up.wait_recv()
-    add(own, part(y), rff.at[0], 0, 112)
-    full_down.wait_recv()
-    add(own, part(y), rff.at[1], 0, 112)
-    here = rows(part(y), 112)
-    stay = load(own.at[here], out.at[here])
-    up = go(own.at[here], out.at[here], dyu)
-    down = go(own.at[here], out.at[here], dyd)
-    up.wait_recv()
-    lo = rows(part(yd), 48)
-    far_up = go(out.at[lo], out.at[lo], dyu)
-    down.wait_recv()
-    hi = rows(part(yu) + 48, 64)
-    far_down = go(out.at[hi], out.at[hi], dyd)
-    far_up.wait_recv()
-    far_down.wait_recv()
+    next(end_two)
+    next(end_one)
+    next(end_two)
+    next(end_one)
+    next(end_two)
     last.wait()
-    stay.wait()
     for cp in go.all:
         if not any(cp is other for other in tails):
             cp.wait_send()
@@ -331,7 +354,7 @@
 def reduce_grads(gexp, gden, cid=1):
     w = gexp.shape[-1]
     low = jnp.bfloat16
-    n = 90
+    n = 100
     return pl.pallas_call(
         reduce_kernel,
         out_shape=jax.ShapeDtypeStruct((464, w), low),
@@ -345,8 +368,10 @@
             pltpu.VMEM((2, 2, 144, w), low),
             pltpu.VMEM((2, 2, 272, w), low),
             pltpu.VMEM((464, w), low),
+            pltpu.VMEM((2, 32, w), low),
             pltpu.VMEM((2, 64, w), low),
-            pltpu.VMEM((2, 112, w), low),
+            pltpu.VMEM((2, 32, w), low),
+            pltpu.VMEM((2, 48, w), low),
             pltpu.VMEM((4, 16, w), low),
             pltpu.SemaphoreType.DMA((n,)),
             pltpu.SemaphoreType.DMA((n,)),
@@ -363,7 +388,8 @@
 LANES = 128
 SLOT_ROWS = 80
 TOKENS = 208
-STEPS = 8
+STEPS = 4
+SPANS = 8
 EPSILON = 1e-06
 LOW = jnp.bfloat16
 F32 = jnp.float32
@@ -425,10 +451,6 @@
             wp[pl.ds(owner * 48 + k * 16, 16), :] = proj_ref[owner, :, pl.ds(k * 768, 768)]
 
 
-def expert_block(ref, e):
-    return ref[:, :, pl.ds(e * 768, 768)].reshape(384, 768)
-
-
 def slots_of(e):
     return pl.ds(e * SLOT_ROWS, SLOT_ROWS)
 
@@ -437,71 +459,137 @@
     return jnp.tanh(0.7978845608028654 * (x + 0.044715 * (x * x * x)))
 
 
-def forward_kernel(
-    at, inputs, received, routes, qkv, proj, router, norms, w_in, w_out, *rest
-):
-    (sent, section_out, c_u, c_nin, c_pro, c_mix, c_res, c_nrm, c_gate, c_slot, c_pre, c_hid, c_result,
-     wp, acc, table_one, table_two) = rest[-17:]
-    step = pl.program_id(0)
-
-    @pl.when(step == 0)
-    def _():
-        u_low = jnp.where(at[1] == 0, inputs[0], received[...])
-        c_u[0] = u_low
-        u = u_low.astype(F32)
-        xhat, _ = norm_parts(u)
-        nin = (xhat * norms[0:1, :] + norms[2:3, :]).astype(LOW)
-        c_nin[0] = nin
-        for k in range(3):
-            cols = pl.ds(k * 768, 768)
-            c_pro[0, :, cols] = mm(nin, qkv[:, :, cols].reshape(768, 768)).astype(LOW)
-        mask = score_mask()
-        low_half = lax.broadcasted_iota(jnp.int32, (TOKENS, LANES), 1) < 64
-        for pair in range(HEADS // 2):
-            q = c_pro[0, :, pl.ds(pair * LANES, LANES)]
-            k = c_pro[0, :, pl.ds(768 + pair * LANES, LANES)]
-            v = c_pro[0, :, pl.ds(1536 + pair * LANES, LANES)]
-            outs = []
-            for half in range(2):
-                qh = jnp.where(low_half if half == 0 else ~low_half, q, jnp.zeros_like(q))
-                scores = jnp.where(mask, mm(qh, k, NT) * 0.125, -1e30)
-                outs.append(mm(soft_parts(scores).astype(LOW), v))
-            c_mix[0, :, pl.ds(pair * LANES, LANES)] = jnp.where(low_half, outs[0], outs[1]).astype(LOW)
-        unpack_proj(proj, wp)
-        residual = u + mm(c_mix[0], wp[...])
-        c_res[0] = residual
-        xhat, _ = norm_parts(residual)
-        normed = (xhat * norms[1:2, :] + norms[3:4, :]).astype(LOW)
-        c_nrm[0] = normed
-        logits = mm(normed, router[...])
-        lane = lax.broadcasted_iota(jnp.int32, (TOKENS, LANES), 1)
-        c_gate[0] = soft_parts(jnp.where(lane < 3, logits, -1e30))
-        one, two, _, _ = route_tables(routes[0])
-        table_one[...] = one
-        table_two[...] = two
-        c_slot[0] = mm(one + two, normed, TN).astype(LOW)
-        acc[...] = jnp.zeros_like(acc)
-
-    for e in range(3):
-        rows = slots_of(e)
-        pre = mm(c_slot[0, rows, :], expert_block(w_in, e), NT)
-        c_pre[0, rows, :] = pre
-        hidden = (0.5 * pre * (1.0 + tanh_part(pre))).astype(LOW)
-        c_hid[0, rows, :] = hidden
-        acc[rows, :] += mm(hidden, expert_block(w_out, e))
-
-    @pl.when(step == STEPS - 1)
-    def _():
-        result = acc[...].astype(LOW)
-        c_result[0] = result
-        lane = lax.broadcasted_iota(jnp.int32, (TOKENS, LANES), 1)
-        gates = c_gate[0]
-        gate_one = jnp.sum(jnp.where(lane == routes[0, :, 0:1], gates, 0.0), axis=1, keepdims=True)
-        gate_two = jnp.sum(jnp.where(lane == routes[0, :, 1:2], gates, 0.0), axis=1, keepdims=True)
-        y = c_res[0] + (mm(table_one[...], result) * gate_one + mm(table_two[...], result) * gate_two)
-        y = y.astype(LOW)
-        sent[...] = y
-        section_out[0] = y[:197]
+def owners_of(j):
+    return pl.ds(j * 4, 4)
+
+
+def columns_of(j):
+    return pl.ds(pl.multiple_of(j * 768, 768), 768)
+
+
+class Weights:
+    def __init__(self, every, experts, qkv, proj, sems):
+        self.every, self.experts, self.qkv, self.proj, self.sems = (every, experts, qkv, proj, sems)
+
+    def dense(self):
+        return (
+            pltpu.make_async_copy(self.every.at[:, pl.ds(384, 48)], self.qkv, self.sems.at[STEPS]),
+            pltpu.make_async_copy(self.every.at[:, pl.ds(432, 16)], self.proj, self.sems.at[STEPS + 1]),
+        )
+
+    def chunk(self, j):
+        return pltpu.make_async_copy(
+            self.every.at[owners_of(j), pl.ds(0, 384)], self.experts.at[owners_of(j)], self.sems.at[j]
+        )
+
+    def start_dense(self):
+        for cp in self.dense():
+            cp.start()
+
+    def wait_dense(self):
+        for cp in self.dense():
+            cp.wait()
+
+    def start_chunks(self):
+        for j in range(STEPS):
+            self.chunk(j).start()
+
+    def block(self, j, which, e):
+        return self.experts[owners_of(j), pl.ds(which * 192, 192), pl.ds(e * 768, 768)].reshape(768, 768)
+
+
+def weight_scratch():
+    return [
+        pltpu.VMEM((16, 384, 2304), LOW),
+        pltpu.VMEM((16, 48, 2304), LOW),
+        pltpu.VMEM((16, 16, 2304), LOW),
+        pltpu.SemaphoreType.DMA((STEPS + 2,)),
+    ]
+
+
+def forward_kernel(at, inputs, received, routes, every, router, norms, *rest):
+    sent, section_out, *outs = rest[-31:-18]
+    (u_at, nin, pro, mix, res, nrm, gate, slot, pre_at, hid, result_at,
+     wp, acc, experts, qkv, proj, sems, out_sems) = rest[-18:]
+    kept = [u_at, nin, pro, mix, res, nrm, gate, slot, pre_at, hid, result_at]
+    micro = at[0]
+    weights = Weights(every, experts, qkv, proj, sems)
+    weights.start_dense()
+    weights.start_chunks()
+
+    def save(n):
+        return pltpu.make_async_copy(kept[n], outs[n].at[micro], out_sems.at[n])
+
+    u_low = jnp.where(at[1] == 0, inputs[0], received[...])
+    u_at[...] = u_low
+    save(0).start()
+    u = u_low.astype(F32)
+    xhat, _ = norm_parts(u)
+    normed_in = (xhat * norms[0:1, :] + norms[2:3, :]).astype(LOW)
+    nin[...] = normed_in
+    save(1).start()
+    one, two, hot_one, hot_two = route_tables(routes[0])
+    weights.wait_dense()
+    for k in range(3):
+        cols = pl.ds(k * 768, 768)
+        pro[:, cols] = mm(normed_in, qkv[:, :, cols].reshape(768, 768)).astype(LOW)
+    save(2).start()
+    mask = score_mask()
+    low_half = lax.broadcasted_iota(jnp.int32, (TOKENS, LANES), 1) < 64
+    for pair in range(HEADS // 2):
+        q = pro[:, pl.ds(pair * LANES, LANES)]
+        k = pro[:, pl.ds(768 + pair * LANES, LANES)]
+        v = pro[:, pl.ds(1536 + pair * LANES, LANES)]
+        sides = []
+        for half in range(2):
+            qh = jnp.where(low_half if half == 0 else ~low_half, q, jnp.zeros_like(q))
+            scores = jnp.where(mask, mm(qh, k, NT) * 0.125, -1e30)
+            sides.append(mm(soft_parts(scores).astype(LOW), v))
+        mix[:, pl.ds(pair * LANES, LANES)] = jnp.where(low_half, sides[0], sides[1]).astype(LOW)
+    save(3).start()
+    unpack_proj(proj, wp)
+    residual = u + mm(mix[...], wp[...])
+    res[...] = residual
+    save(4).start()
+    xhat, _ = norm_parts(residual)
+    normed = (xhat * norms[1:2, :] + norms[3:4, :]).astype(LOW)
+    nrm[...] = normed
+    save(5).start()
+    logits = mm(normed, router[...])
+    lane = lax.broadcasted_iota(jnp.int32, (TOKENS, LANES), 1)
+    gates = soft_parts(jnp.where(lane < 3, logits, -1e30))
+    gate[...] = gates
+    save(6).start()
+    slot[...] = mm(one + two, normed, TN).astype(LOW)
+    save(7).start()
+    acc[...] = jnp.zeros_like(acc)
+
+    def step(j, carry):
+        weights.chunk(j).wait()
+        cols = columns_of(j)
+        for e in range(3):
+            rows = slots_of(e)
+            pre = mm(slot[rows, :], weights.block(j, 0, e), NT)
+            pre_at[rows, cols] = pre
+            hidden = (0.5 * pre * (1.0 + tanh_part(pre))).astype(LOW)
+            hid[rows, cols] = hidden
+            acc[rows, :] += mm(hidden, weights.block(j, 1, e))
+        return carry
+
+    lax.fori_loop(0, STEPS, step, 0)
+    save(8).start()
+    save(9).start()
+    result = acc[...].astype(LOW)
+    result_at[...] = result
+    save(10).start()
+    gate_one = jnp.sum(gates * hot_one, axis=1, keepdims=True)
+    gate_two = jnp.sum(gates * hot_two, axis=1, keepdims=True)
+    y = res[...] + (mm(one, result) * gate_one + mm(two, result) * gate_two)
+    y = y.astype(LOW)
+    sent[...] = y
+    section_out[0] = y[:197]
+    for n in range(11):
+        save(n).wait()
 
 
 def whole(shape):
@@ -512,18 +600,7 @@
     return pl.BlockSpec((1,) + shape[1:], lambda j, at: (at[0],) + (0,) * (len(shape) - 1))
 
 
-def chunk(shape):
-    return pl.BlockSpec((1, shape[1], 384), lambda j, at: (at[0], 0, j))
-
-
-def fixed(shape, index):
-    return pl.BlockSpec(shape, lambda j, at: index)
-
-
-WEIGHT_IN = pl.BlockSpec((2, 192, 2304), lambda j, at: (j, 0, 0))
-WEIGHT_OUT = pl.BlockSpec((2, 192, 2304), lambda j, at: (j, 1, 0))
-QKV = fixed((16, 48, 2304), (0, 8, 0))
-PROJ = fixed((16, 16, 2304), (0, 27, 0))
+ANYWHERE = pl.BlockSpec(memory_space=pl.ANY)
 CACHE = [
     ((2, 197, 768), LOW),
     ((2, TOKENS, 768), LOW),
@@ -549,10 +626,6 @@
 ]
 
 
-def held(shape):
-    return chunk(shape) if shape[-1] == 3072 else by_micro(shape)
-
-
 def call_tick(body, at, operands, specs, kept, kinds, scratch, flops):
     grown = list(operands)
     grown_specs = list(specs)
@@ -561,17 +634,20 @@
         for n, array in enumerate(kept):
             aliases[1 + len(grown)] = 1 + n
             grown.append(array)
-            grown_specs.append(pl.BlockSpec(memory_space=pl.ANY))
+            grown_specs.append(ANYWHERE)
     return pl.pallas_call(
         body,
         out_shape=[jax.ShapeDtypeStruct((TOKENS, 768), LOW)]
         + [jax.ShapeDtypeStruct(shape, kind) for shape, kind in kinds],
         grid_spec=pltpu.PrefetchScalarGridSpec(
             num_scalar_prefetch=1,
-            grid=(STEPS,),
+            grid=(1,),
             in_specs=grown_specs,
-            out_specs=[whole((TOKENS, 768))] + [held(shape) for shape, _ in kinds],
-            scratch_shapes=scratch,
+            out_specs=[whole((TOKENS, 768)), by_micro(kinds[0][0])] + [ANYWHERE] * (len(kinds) - 1),
+            scratch_shapes=[pltpu.VMEM(shape[1:], kind) for shape, kind in kinds[1:]]
+            + scratch
+            + weight_scratch()
+            + [pltpu.SemaphoreType.DMA((len(kinds),))],
         ),
         input_output_aliases=aliases,
         compiler_params=pltpu.CompilerParams(vmem_limit_bytes=60 * 1024 * 1024),
@@ -583,143 +659,156 @@
     outs = call_tick(
         forward_kernel,
         at,
-        [inputs, received, routes, every, every, router, norms, every, every],
+        [inputs, received, routes, every, router, norms],
         [
-            by_micro(inputs.shape), whole((TOKENS, 768)), by_micro(routes.shape), QKV, PROJ,
-            whole(router.shape), whole(norms.shape), WEIGHT_IN, WEIGHT_OUT,
+            by_micro(inputs.shape), whole((TOKENS, 768)), by_micro(routes.shape), ANYWHERE,
+            whole(router.shape), whole(norms.shape),
         ],
         kept,
         CACHE,
-        [
-            pltpu.VMEM((768, 768), LOW),
-            pltpu.VMEM((256, 768), F32),
-            pltpu.VMEM((TOKENS, 256), LOW),
-            pltpu.VMEM((TOKENS, 256), LOW),
-        ],
+        [pltpu.VMEM((768, 768), LOW), pltpu.VMEM((256, 768), F32)],
         4_000_000_000,
     )
     return outs[0], outs[1:]
 
 
 def backward_kernel(
-    at, cotangent, returned, routes, qkv, proj, router, norms, w_in, w_out,
-    c_u, c_pro, c_res, c_gate, c_pre, c_result, *rest
+    at, cotangent, returned, routes, every, router, norms, gate, result, h_u, h_pro, h_res, h_pre, *rest
 ):
-    (sent, section_in_grad, b_gres, b_gpre, b_ga, b_gp, b_gl, b_norm,
-     wp, acc, table, grad_normed_part) = rest[-12:]
-    step = pl.program_id(0)
-
-    def grad_y():
-        return jnp.where(at[1] == 1, cotangent[0], returned[...]).astype(F32)
-
-    @pl.when(step == 0)
-    def _():
-        gy = grad_y()
-        one, two, hot_one, hot_two = route_tables(routes[0])
-        table[...] = one + two
-        gates = c_gate[0]
-        gate_one = jnp.sum(gates * hot_one, axis=1, keepdims=True)
-        gate_two = jnp.sum(gates * hot_two, axis=1, keepdims=True)
-        b_gres[0] = (
-            mm(one, (gy * gate_one).astype(LOW), TN) + mm(two, (gy * gate_two).astype(LOW), TN)
-        ).astype(LOW)
-        result = c_result[0]
-        pick_one = jnp.sum(gy * mm(one, result), axis=1, keepdims=True)
-        pick_two = jnp.sum(gy * mm(two, result), axis=1, keepdims=True)
-        grad_gates = hot_one * pick_one + hot_two * pick_two
-        grad_logits = (
-            gates * (grad_gates - jnp.sum(grad_gates * gates, axis=1, keepdims=True))
-        ).astype(LOW)
-        b_gl[0] = grad_logits
-        grad_normed_part[...] = mm(grad_logits, router[...], NT)
-        acc[...] = jnp.zeros_like(acc)
-
-    for e in range(3):
-        rows = slots_of(e)
-        grad_hidden = mm(b_gres[0, rows, :], expert_block(w_out, e), NT)
-        x = c_pre[0, rows, :]
-        t = tanh_part(x)
-        slope = 0.5 * (1.0 + t) + 0.5 * x * (1.0 - t * t) * (
-            0.7978845608028654 * (1.0 + 3 * 0.044715 * (x * x))
-        )
-        grad_pre = (slope * grad_hidden).astype(LOW)
-        b_gpre[0, rows, :] = grad_pre
-        acc[rows, :] += mm(grad_pre, expert_block(w_in, e))
-
-    @pl.when(step == STEPS - 1)
-    def _():
-        grad_normed = mm(table[...], acc[...].astype(LOW)) + grad_normed_part[...]
-        xhat, rstd = norm_parts(c_res[0])
-        b_norm[0, 1:2, :] = jnp.sum(grad_normed * xhat, axis=0, keepdims=True)
-        b_norm[0, 3:4, :] = jnp.sum(grad_normed, axis=0, keepdims=True)
-        b_norm[0, 4:8, :] = jnp.zeros((4, 768), F32)
-        grad_residual = grad_y() + norm_back(grad_normed, xhat, rstd, norms[1:2, :])
-        ga = grad_residual.astype(LOW)
-        b_ga[0] = ga
-        unpack_proj(proj, wp)
-        grad_mixed = mm(ga, wp[...], NT).astype(LOW)
-        mask = score_mask()
-        low_half = lax.broadcasted_iota(jnp.int32, (TOKENS, LANES), 1) < 64
-        for pair in range(HEADS // 2):
-            q = c_pro[0, :, pl.ds(pair * LANES, LANES)]
-            k = c_pro[0, :, pl.ds(768 + pair * LANES, LANES)]
-            v = c_pro[0, :, pl.ds(1536 + pair * LANES, LANES)]
-            gm = grad_mixed[:, pair * LANES:(pair + 1) * LANES]
-            gq, gk, gv = [], [], []
-            for half in range(2):
-                keep = low_half if half == 0 else ~low_half
-                qh = jnp.where(keep, q, jnp.zeros_like(q))
-                gh = jnp.where(keep, gm, jnp.zeros_like(gm))
-                probs = soft_parts(jnp.where(mask, mm(qh, k, NT) * 0.125, -1e30))
-                grad_probs = mm(gh, v, NT)
-                gs = (
-                    probs * (grad_probs - jnp.sum(grad_probs * probs, axis=-1, keepdims=True))
-                ).astype(LOW)
-                gq.append(mm(gs, k))
-                gk.append(mm(gs, q, TN))
-                gv.append(mm(probs.astype(LOW), gm, TN))
-            b_gp[0, :, pl.ds(pair * LANES, LANES)] = (jnp.where(low_half, gq[0], gq[1]) * 0.125).astype(LOW)
-            b_gp[0, :, pl.ds(768 + pair * LANES, LANES)] = (jnp.where(low_half, gk[0], gk[1]) * 0.125).astype(LOW)
-            b_gp[0, :, pl.ds(1536 + pair * LANES, LANES)] = jnp.where(low_half, gv[0], gv[1]).astype(LOW)
-        grad_nin = jnp.zeros((TOKENS, 768), F32)
-        for k in range(3):
-            cols = pl.ds(k * 768, 768)
-            grad_nin = grad_nin + mm(b_gp[0, :, cols], qkv[:, :, cols].reshape(768, 768), NT)
-        xhat, rstd = norm_parts(c_u[0].astype(F32))
-        b_norm[0, 0:1, :] = jnp.sum(grad_nin * xhat, axis=0, keepdims=True)
-        b_norm[0, 2:3, :] = jnp.sum(grad_nin, axis=0, keepdims=True)
-        grad_in = grad_residual + norm_back(grad_nin, xhat, rstd, norms[0:1, :])
-        section_in_grad[0] = grad_in[:197]
-        sent[...] = grad_in.astype(LOW)
+    sent, section_in_grad, *outs = rest[-26:-18]
+    (gres, gpre, ga_at, gp, gl, gnorm,
+     wp, acc, u_at, pro, res, pre_at, in_sems, experts, qkv, proj, sems, out_sems) = rest[-18:]
+    kept = [gres, gpre, ga_at, gp, gl, gnorm]
+    micro = at[0]
+    weights = Weights(every, experts, qkv, proj, sems)
+    sources, targets = (h_pre, h_res, h_pro, h_u), (pre_at, res, pro, u_at)
+
+    def fetch(n):
+        return pltpu.make_async_copy(sources[n].at[micro], targets[n], in_sems.at[n])
+
+    def save(n):
+        return pltpu.make_async_copy(kept[n], outs[n].at[micro], out_sems.at[n])
+
+    fetch(0).start()
+    weights.start_chunks()
+    weights.start_dense()
+    for n in range(1, 4):
+        fetch(n).start()
+    gy = jnp.where(at[1] == 1, cotangent[0], returned[...]).astype(F32)
+    one, two, hot_one, hot_two = route_tables(routes[0])
+    gates = gate[0]
+    gate_one = jnp.sum(gates * hot_one, axis=1, keepdims=True)
+    gate_two = jnp.sum(gates * hot_two, axis=1, keepdims=True)
+    gres[...] = (
+        mm(one, (gy * gate_one).astype(LOW), TN) + mm(two, (gy * gate_two).astype(LOW), TN)
+    ).astype(LOW)
+    save(0).start()
+    pick_one = jnp.sum(gy * mm(one, result[0]), axis=1, keepdims=True)
+    pick_two = jnp.sum(gy * mm(two, result[0]), axis=1, keepdims=True)
+    grad_gates = hot_one * pick_one + hot_two * pick_two
+    grad_logits = (
+        gates * (grad_gates - jnp.sum(grad_gates * gates, axis=1, keepdims=True))
+    ).astype(LOW)
+    gl[...] = grad_logits
+    save(4).start()
+    acc[...] = jnp.zeros_like(acc)
+    fetch(0).wait()
+
+    def step(j, carry):
+        weights.chunk(j).wait()
+        cols = columns_of(j)
+        for e in range(3):
+            rows = slots_of(e)
+            grad_hidden = mm(gres[rows, :], weights.block(j, 1, e), NT)
+            x = pre_at[rows, cols]
+            t = tanh_part(x)
+            slope = 0.5 * (1.0 + t) + 0.5 * x * (1.0 - t * t) * (
+                0.7978845608028654 * (1.0 + 3 * 0.044715 * (x * x))
+            )
+            grad_pre = (slope * grad_hidden).astype(LOW)
+            gpre[rows, cols] = grad_pre
+            acc[rows, :] += mm(grad_pre, weights.block(j, 0, e))
+        return carry
+
+    lax.fori_loop(0, STEPS, step, 0)
+    save(1).start()
+    weights.wait_dense()
+    for n in range(1, 4):
+        fetch(n).wait()
+    grad_normed = mm(one + two, acc[...].astype(LOW)) + mm(grad_logits, router[...], NT)
+    xhat, rstd = norm_parts(res[...])
+    gnorm[1:2, :] = jnp.sum(grad_normed * xhat, axis=0, keepdims=True)
+    gnorm[3:4, :] = jnp.sum(grad_normed, axis=0, keepdims=True)
+    gnorm[4:8, :] = jnp.zeros((4, 768), F32)
+    grad_residual = gy + norm_back(grad_normed, xhat, rstd, norms[1:2, :])
+    ga = grad_residual.astype(LOW)
+    ga_at[...] = ga
+    save(2).start()
+    unpack_proj(proj, wp)
+    grad_mixed = mm(ga, wp[...], NT).astype(LOW)
+    mask = score_mask()
+    low_half = lax.broadcasted_iota(jnp.int32, (TOKENS, LANES), 1) < 64
+    for pair in range(HEADS // 2):
+        q = pro[:, pl.ds(pair * LANES, LANES)]
+        k = pro[:, pl.ds(768 + pair * LANES, LANES)]
+        v = pro[:, pl.ds(1536 + pair * LANES, LANES)]
+        gm = grad_mixed[:, pair * LANES:(pair + 1) * LANES]
+        gq, gk, gv = [], [], []
+        for half in range(2):
+            keep = low_half if half == 0 else ~low_half
+            qh = jnp.where(keep, q, jnp.zeros_like(q))
+            gh = jnp.where(keep, gm, jnp.zeros_like(gm))
+            probs = soft_parts(jnp.where(mask, mm(qh, k, NT) * 0.125, -1e30))
+            grad_probs = mm(gh, v, NT)
+            gs = (
+                probs * (grad_probs - jnp.sum(grad_probs * probs, axis=-1, keepdims=True))
+            ).astype(LOW)
+            gq.append(mm(gs, k))
+            gk.append(mm(gs, q, TN))
+            gv.append(mm(probs.astype(LOW), gm, TN))
+        gp[:, pl.ds(pair * LANES, LANES)] = (jnp.where(low_half, gq[0], gq[1]) * 0.125).astype(LOW)
+        gp[:, pl.ds(768 + pair * LANES, LANES)] = (jnp.where(low_half, gk[0], gk[1]) * 0.125).astype(LOW)
+        gp[:, pl.ds(1536 + pair * LANES, LANES)] = jnp.where(low_half, gv[0], gv[1]).astype(LOW)
+    save(3).start()
+    grad_nin = jnp.zeros((TOKENS, 768), F32)
+    for k in range(3):
+        cols = pl.ds(k * 768, 768)
+        grad_nin = grad_nin + mm(gp[:, cols], qkv[:, :, cols].reshape(768, 768), NT)
+    xhat, rstd = norm_parts(u_at[...].astype(F32))
+    gnorm[0:1, :] = jnp.sum(grad_nin * xhat, axis=0, keepdims=True)
+    gnorm[2:3, :] = jnp.sum(grad_nin, axis=0, keepdims=True)
+    save(5).start()
+    grad_in = grad_residual + norm_back(grad_nin, xhat, rstd, norms[0:1, :])
+    section_in_grad[0] = grad_in[:197]
+    sent[...] = grad_in.astype(LOW)
+    for n in range(6):
+        save(n).wait()
 
 
 def backward_tick(at, cotangent, returned, routes, every, router, norms, caches, kept):
     _, c_u, _, c_pro, _, c_res, _, c_gate, _, c_pre, _, c_result = caches
-    mine = [c_u, c_pro, c_res, c_gate, c_pre, c_result]
     outs = call_tick(
         backward_kernel,
         at,
-        [cotangent, returned, routes, every, every, router, norms, every, every] + mine,
+        [cotangent, returned, routes, every, router, norms, c_gate, c_result, c_u, c_pro, c_res, c_pre],
         [
-            by_micro(cotangent.shape), whole((TOKENS, 768)), by_micro(routes.shape), QKV, PROJ,
-            whole(router.shape), whole(norms.shape), WEIGHT_IN, WEIGHT_OUT,
+            by_micro(cotangent.shape), whole((TOKENS, 768)), by_micro(routes.shape), ANYWHERE,
+            whole(router.shape), whole(norms.shape), by_micro(c_gate.shape), by_micro(c_result.shape),
         ]
-        + [held(array.shape) for array in mine],
+        + [ANYWHERE] * 4,
         kept,
         BACK,
-        [
-            pltpu.VMEM((768, 768), LOW),
-            pltpu.VMEM((256, 768), F32),
-            pltpu.VMEM((TOKENS, 256), LOW),
-            pltpu.VMEM((TOKENS, 768), F32),
-        ],
+        [pltpu.VMEM((768, 768), LOW), pltpu.VMEM((256, 768), F32)]
+        + [pltpu.VMEM(array.shape[1:], array.dtype) for array in (c_u, c_pro, c_res, c_pre)]
+        + [pltpu.SemaphoreType.DMA((4,))],
         6_000_000_000,
     )
     return outs[0], outs[1:]
 
 
-def weight_kernel(c_nin, c_mix, c_nrm, c_slot, c_hid, b_gres, b_gpre, b_ga, b_gp, b_gl, b_norm, gexp, gden):
+def weight_kernel(c_nin, c_mix, c_nrm, c_slot, c_hid, b_gres, b_gpre, b_ga, b_gp, b_gl, b_norm, gexp, gden, held_grads, sems):
     step = pl.program_id(0)
+    pair = pl.ds(step * 2, 2)
 
     def both(ref, rows=None):
         if rows is None:
@@ -732,8 +821,9 @@
         first = mm(both(b_gpre, rows), both(c_slot, rows), TN).astype(LOW)
         second = mm(both(c_hid, rows), both(b_gres, rows), TN).astype(LOW)
         for owner in range(2):
-            gexp[owner, pl.ds(0, 192), cols] = first[owner * 192:(owner + 1) * 192]
-            gexp[owner, pl.ds(192, 192), cols] = second[owner * 192:(owner + 1) * 192]
+            held_grads[step * 2 + owner, pl.ds(0, 192), cols] = first[owner * 192:(owner + 1) * 192]
+            held_grads[step * 2 + owner, pl.ds(192, 192), cols] = second[owner * 192:(owner + 1) * 192]
+    pltpu.make_async_copy(held_grads.at[pair], gexp.at[pair], sems.at[step]).start()
 
     for k in range(3):
         @pl.when(step == k)
@@ -741,7 +831,7 @@
             cols = pl.ds(k * 768, 768)
             grad = mm(both(c_nin), jnp.concatenate([b_gp[0, :, cols], b_gp[1, :, cols]], axis=0), TN).astype(LOW)
             for owner in range(16):
-                gden[owner, pl.ds(0, 48), cols] = grad[owner * 48:(owner + 1) * 48]
+                gden[owner, pl.ds(32, 48), cols] = grad[owner * 48:(owner + 1) * 48]
 
     @pl.when(step == 3)
     def _():
@@ -749,15 +839,21 @@
         for owner in range(16):
             for k in range(3):
                 at = owner * 48 + k * 16
-                gden[owner, pl.ds(48, 16), pl.ds(k * 768, 768)] = grad[at:at + 16]
+                gden[owner, pl.ds(16, 16), pl.ds(k * 768, 768)] = grad[at:at + 16]
 
     @pl.when(step == 4)
     def _():
         router = mm(both(b_gl), both(c_nrm), TN)[:8]
         small = jnp.concatenate([router, b_norm[0] + b_norm[1]], axis=0).astype(LOW)
         for owner in range(16):
-            gden[owner, pl.ds(64, 16), pl.ds(0, 768)] = small
-            gden[owner, pl.ds(64, 16), pl.ds(768, 1536)] = jnp.zeros((16, 1536), LOW)
+            gden[owner, pl.ds(0, 16), pl.ds(0, 768)] = small
+            gden[owner, pl.ds(0, 16), pl.ds(768, 1536)] = jnp.zeros((16, 1536), LOW)
+
+    @pl.when(step == SPANS - 1)
+    def _():
+        for k in range(SPANS):
+            done = pl.ds(k * 2, 2)
+            pltpu.make_async_copy(held_grads.at[done], gexp.at[done], sems.at[k]).wait()
 
 
 def weight_grads(caches, backs):
@@ -776,14 +872,34 @@
             jax.ShapeDtypeStruct((16, 384, 2304), LOW),
             jax.ShapeDtypeStruct((16, 80, 2304), LOW),
         ],
-        grid=(STEPS,),
+        grid=(SPANS,),
         in_specs=[spec(array.shape) for array in operands],
         out_specs=[
-            pl.BlockSpec((2, 384, 2304), lambda j: (j, 0, 0)),
+            pl.BlockSpec(memory_space=pl.ANY),
             pl.BlockSpec((16, 80, 2304), lambda j: (0, 0, 0)),
         ],
+        scratch_shapes=[pltpu.VMEM((16, 384, 2304), LOW), pltpu.SemaphoreType.DMA((SPANS,))],
         compiler_params=pltpu.CompilerParams(vmem_limit_bytes=60 * 1024 * 1024),
     )(*operands)
+
+
+def spread_kernel(total, g_in, g_out, g_qkv, g_proj, small):
+    for e in range(3):
+        cols = pl.ds(e * 768, 768)
+        g_in[0, :, e, :] = total[pl.ds(80, 192), cols].astype(F32)
+        g_out[0, :, e, :] = total[pl.ds(272, 192), cols].astype(F32)
+        g_proj[0, pl.ds(e * 16, 16), :] = total[pl.ds(16, 16), cols].astype(F32)
+    g_qkv[0] = total[pl.ds(32, 48), :].astype(F32)
+    small[...] = total[pl.ds(0, 16), pl.ds(0, 768)].astype(F32)
+
+
+def spread(total):
+    shapes = [(1, 192, 3, 768), (1, 192, 3, 768), (1, 48, 2304), (1, 48, 768), (16, 768)]
+    return pl.pallas_call(
+        spread_kernel,
+        out_shape=[jax.ShapeDtypeStruct(shape, F32) for shape in shapes],
+        compiler_params=pltpu.CompilerParams(vmem_limit_bytes=60 * 1024 * 1024),
+    )(total)
 
 
 def to_section(value, by):
@@ -829,18 +945,19 @@
         if tick < 2:
             returned = to_section(sent, -1)
     gexp, gden = weight_grads(caches, backs)
-    total = reduce_grads(gexp.reshape(2, 4, 2, 384, 2304), gden.reshape(2, 4, 2, 80, 2304)).astype(F32)
-    mine = lax.dynamic_slice_in_dim(total[448:, :768], lax.axis_index("shard") * 48, 48, axis=1)
+    total = reduce_grads(gexp.reshape(2, 4, 2, 384, 2304), gden.reshape(2, 4, 2, 80, 2304))
+    g_in, g_out, g_qkv, g_proj, small = spread(total)
+    mine = lax.dynamic_slice_in_dim(small, lax.axis_index("shard") * 48, 48, axis=1)
     return (
         caches[0][None, :, None],
         backs[0][None, :, None],
         mine[8:10][None],
         mine[10:12][None],
-        total[384:432][None],
-        total[432:448].reshape(16, 3, 768).transpose(1, 0, 2).reshape(1, 48, 768),
+        g_qkv,
+        g_proj,
         mine[:3].T[None],
-        total[:192].reshape(1, 192, 3, 768),
-        total[192:384].reshape(1, 192, 3, 768),
+        g_in,
+        g_out,
     )
 
 

time: 544 us -> 482 us (0.89)
  Pallas kernels: 451 us -> 404 us
  local copies, waits for them, and re-layouts: 37.2 us -> 25.6 us
    pallas_call x1, Pallas kernels: 162 us -> 133 us  [reduce_grads(): pl.pallas_call(reduce_kernel, out_shape=jax.ShapeDtypeStruct((464, w), lo...]
    pallas_call x6, Pallas kernels: 171 us -> 148 us  [call_tick(): pl.pallas_call(body, out_shape=[jax.ShapeDtypeStruct((TOKENS, 768), LOW)]...]
    reshape x3 -> x0, local copies, waits for them, and re-layouts: 6.94 us -> none  [the longest x1 4.07 us: local(): total[192:384].reshape(1, 192, 3, 768)]
where the time goes in v2:
time: 482 us; the launch traced here: 474 us
  Pallas kernels  404 us (84%)
  waiting for transfers between devices  26.2 us (5%)
  local copies, waits for them, and re-layouts  25.6 us (5%)
  starting transfers between devices  13.4 us (3%)
    pallas_call x6, Pallas kernels, call_tick(): pl.pallas_call(body, out_shape=[jax.ShapeDtypeStruct((TOKENS, 768), LOW)]...  148 us
    pallas_call x1, Pallas kernels, reduce_grads(): pl.pallas_call(reduce_kernel, out_shape=jax.ShapeDtypeStruct((464, w), lo...  133 us
    pallas_call x1, Pallas kernels, gather(): pl.pallas_call(body, out_shape=jax.ShapeDtypeStruct((2, 4, 2, r, w), own....  97.2 us
    ppermute x4, waiting for transfers between devices, to_section(): return lax.ppermute(value, 'section', pairs)  26.2 us
    pallas_call x1, Pallas kernels, weight_grads(): pl.pallas_call(weight_kernel, out_shape=[jax.ShapeDtypeStruct((16, 384, 2...  21.2 us
    unnamed x52, local copies, waits for them, and re-layouts  18.1 us
    ppermute x4, starting transfers between devices, to_section(): return lax.ppermute(value, 'section', pairs)  13.4 us
  transfers between devices with their start and end apart: 4, of which 4 were waited for; matrix products, arithmetic and copies ran while one was open for 1% of the time, Pallas kernels for 0%

profile of v2, /device:TPU:1, one launch (start us, length us, event | category | flops | bytes accessed | tf_op | source)
XLA Modules:
  0.0 474.3 jit_solution(56364934440300783)
XLA Ops:
  0.6 1.9 copy.77
  5.5 1.3 copy-done.2
  6.9 97.2 %shard_map.169 = bf16[2,4,2,464,2304]{4,3,2,1,0:T(8,128)(2,1)} custom-call(bf16[464,2304]{1,0:T(8,128)(2,1)} %copy-done.2), custom_call_target="tpu_custom_call" | custom-call | tf_op jit(solution)/shard_map/pallas_call | solution.py:150
  109.8 19.4 %shard_map.170 = (bf16[208,768]{1,0:T(8,128)(2,1)}, bf16[2,197,768]{2,1,0:T(8,128)(2,1)}, bf16[2,208,768]{2,1,0:T(8,128)(2,1)}, bf16[2,208,768]{2,1,0:T(8,128)(2...) custom-call(s32[2]{0:T(128)} %pad_add_fusion.2.at, ...), custom_call_target="tpu_custom_call" | custom-call | flops 4000000000 | bytes 40000000 | tf_op jit(solution)/shard_map/pallas_call | solution.py:638
  129.3 4.9 %collective-permute-start = (bf16[208,768]{1,0:T(8,128)(2,1)}, bf16[208,768]{1,0:T(8,128)(2,1)S(1)}, u32[]{:S(2)}, u32[]{:S(2)}) collective-permute-start(bf16[208,768]{1,0:T(8,128)(2,1)} %get-tuple-element.77), channel_id=1, source_target_pairs={{0,64},{1,65},{2,66},{3,67},{4,68},{5,69},{6,70},{7,71},{8,72},{9,... | collective-permute-start | bytes 958472 | tf_op jit(solution)/shard_map/ppermute | solution.py:907
  134.7 6.4 %collective-permute-done.received = bf16[208,768]{1,0:T(8,128)(2,1)S(1)} collective-permute-done((bf16[208,768]{1,0:T(8,128)(2,1)}, bf16[208,768]{1,0:T(8,128)(2,1)S(1)}, u32[]{:S(2)}, u32[]{:S(2)}) %collective-permute-start) | collective-permute-done | bytes 319520 | tf_op jit(solution)/shard_map/ppermute | solution.py:907
  141.9 19.5 %shard_map.171 = (bf16[208,768]{1,0:T(8,128)(2,1)}, bf16[2,197,768]{2,1,0:T(8,128)(2,1)}, bf16[2,208,768]{2,1,0:T(8,128)(2,1)}, bf16[2,208,768]{2,1,0:T(8,128)(2...) custom-call(s32[2]{0:T(128)} %pad_add_fusion.1.at, ...), custom_call_target="tpu_custom_call", output_to_operand_aliasing={{1}: (7, {}), {2}: (8, {}), {3}: (9, {}), {4}: (10, {}), {5... | custom-call | flops 4000000000 | bytes 40000000 | tf_op jit(solution)/shard_map/pallas_call | solution.py:638
  161.4 5.5 %collective-permute-start.1 = (bf16[208,768]{1,0:T(8,128)(2,1)}, bf16[208,768]{1,0:T(8,128)(2,1)S(1)}, u32[]{:S(2)}, u32[]{:S(2)}) collective-permute-start(bf16[208,768]{1,0:T(8,128)(2,1)} %get-tuple-element.90), channel_id=1, source_target_pairs={{0,64},{1,65},{2,66},{3,67},{4,68},{5,69},{6,70},{7,71},{8,72},{9,... | collective-permute-start | bytes 958472 | tf_op jit(solution)/shard_map/ppermute | solution.py:907
  169.1 4.2 collective-permute-done.1.received
  174.0 19.8 %shard_map.172 = (bf16[208,768]{1,0:T(8,128)(2,1)}, bf16[2,197,768]{2,1,0:T(8,128)(2,1)}, bf16[2,208,768]{2,1,0:T(8,128)(2,1)}, bf16[2,208,768]{2,1,0:T(8,128)(2...) custom-call(s32[2]{0:T(128)} %pad_add_fusion.at, ...), custom_call_target="tpu_custom_call", output_to_operand_aliasing={{1}: (7, {}), {2}: (8, {}), {3}: (9, {}), {4}: (10, {}), {5... | custom-call | flops 4000000000 | bytes 40000000 | tf_op jit(solution)/shard_map/pallas_call | solution.py:638
  193.8 27.1 %shard_map.173 = (bf16[208,768]{1,0:T(8,128)(2,1)}, f32[2,197,768]{2,1,0:T(8,128)}, bf16[2,256,768]{2,1,0:T(8,128)(2,1)}, bf16[2,240,3072]{2,1,0:T(8,128)(2,1)},...) custom-call(s32[2]{0:T(128)} %pad_add_fusion.5.at, ...), custom_call_target="tpu_custom_call" | custom-call | flops 6000000000 | bytes 40000000 | tf_op jit(solution)/shard_map/pallas_call | solution.py:638
  221.0 1.5 collective-permute-start.2
  223.0 8.9 %collective-permute-done.2.returned = bf16[208,768]{1,0:T(8,128)(2,1)S(1)} collective-permute-done((bf16[208,768]{1,0:T(8,128)(2,1)}, bf16[208,768]{1,0:T(8,128)(2,1)S(1)}, u32[]{:S(2)}, u32[]{:S(2)}) %collective-permute-start.2) | collective-permute-done | bytes 319520 | tf_op jit(solution)/shard_map/ppermute | solution.py:907
  232.7 31.3 %shard_map.174 = (bf16[208,768]{1,0:T(8,128)(2,1)}, f32[2,197,768]{2,1,0:T(8,128)}, bf16[2,256,768]{2,1,0:T(8,128)(2,1)}, bf16[2,240,3072]{2,1,0:T(8,128)(2,1)},...) custom-call(s32[2]{0:T(128)} %pad_add_fusion.4.at, ...), custom_call_target="tpu_custom_call", output_to_operand_aliasing={{1}: (13, {}), {2}: (14, {}), {3}: (15, {}), {4}: (16, {}),... | custom-call | flops 6000000000 | bytes 40000000 | tf_op jit(solution)/shard_map/pallas_call | solution.py:638
  263.9 1.5 collective-permute-start.3
  267.3 6.6 %collective-permute-done.3.returned = bf16[208,768]{1,0:T(8,128)(2,1)S(1)} collective-permute-done((bf16[208,768]{1,0:T(8,128)(2,1)}, bf16[208,768]{1,0:T(8,128)(2,1)S(1)}, u32[]{:S(2)}, u32[]{:S(2)}) %collective-permute-start.3) | collective-permute-done | bytes 319520 | tf_op jit(solution)/shard_map/ppermute | solution.py:907
  274.7 31.1 %shard_map.175 = (bf16[208,768]{1,0:T(8,128)(2,1)}, f32[2,197,768]{2,1,0:T(8,128)}, bf16[2,256,768]{2,1,0:T(8,128)(2,1)}, bf16[2,240,3072]{2,1,0:T(8,128)(2,1)},...) custom-call(s32[2]{0:T(128)} %pad_add_fusion.3.at, ...), custom_call_target="tpu_custom_call", output_to_operand_aliasing={{1}: (13, {}), {2}: (14, {}), {3}: (15, {}), {4}: (16, {}),... | custom-call | flops 6000000000 | bytes 40000000 | tf_op jit(solution)/shard_map/pallas_call | solution.py:638
  305.8 21.2 %shard_map.176 = (bf16[16,384,2304]{2,1,0:T(8,128)(2,1)}, bf16[16,80,2304]{2,1,0:T(8,128)(2,1)}) custom-call(bf16[2,208,768]{2,1,0:T(8,128)(2,1)} %get-tuple-element.127.c_nin, bf16[2,208,768]{2,1,0:T(8,128)(2,1)} %get-tuple-element.128.c_mix, bf16[2,208,768]{2,1,0:T(8,128)(2,1)} %get-tuple-element.129.c_nrm, ...), custom_call_target="tpu_custom_call" | custom-call | tf_op jit(solution)/shard_map/pallas_call | solution.py:869
  327.0 132.5 %shard_map.177.total = bf16[464,2304]{1,0:T(8,128)(2,1)} custom-call(bf16[2,4,2,384,2304]{4,3,2,1,0:T(8,128)(2,1)} %bitcast.55, bf16[2,4,2,80,2304]{4,3,2,1,0:T(8,128)(2,1)} %bitcast.57), custom_call_target="tpu_custom_call" | custom-call | tf_op jit(solution)/shard_map/pallas_call | solution.py:358
  459.6 4.4 shard_map.178
  463.9 3.4 copy.86
  467.3 1.5 copy.87
  470.2 2.3 copy.84
  472.4 1.4 dynamic-slice_bitcast_fusion.1
  (68 shorter events, 18.0 us)
Async XLA Ops:
  2.6 1.2 copy-start.4
  3.8 0.9 copy-start.12
  3.8 1.0 copy-start.14
  3.8 1.0 copy-start.15
  3.8 1.0 copy-start.16
  4.5 0.9 copy-start.11
  5.5 1.3 copy-start.2
  6.8 99.1 %copy-start.13 = (s32[1,2,1,197,2]{3,4,2,1,0:T(2,128)S(1)}, s32[1,2,1,197,2]{3,4,2,1,0:T(2,128)}, u32[]{:S(2)}) copy-start(s32[1,2,1,197,2]{3,4,2,1,0:T(2,128)} %param.12) | copy-start | bytes 9460
  6.8 99.2 %copy-start.5 = (bf16[2,1,197,768]{3,0,2,1:T(2,128)(2,1)S(1)}, bf16[2,1,197,768]{3,0,2,1:T(2,128)(2,1)}, u32[]{:S(2)}) copy-start(bf16[2,1,197,768]{3,0,2,1:T(2,128)(2,1)} %param.10) | copy-start | bytes 1815556
  129.3 11.9 %collective-permute-start = (bf16[208,768]{1,0:T(8,128)(2,1)}, bf16[208,768]{1,0:T(8,128)(2,1)S(1)}, u32[]{:S(2)}, u32[]{:S(2)}) collective-permute-start(bf16[208,768]{1,0:T(8,128)(2,1)} %get-tuple-element.77), channel_id=1, source_target_pairs={{0,64},{1,65},{2,66},{3,67},{4,68},{5,69},{6,70},{7,71},{8,72},{9,... | collective-permute-start | bytes 958472 | tf_op jit(solution)/shard_map/ppermute | solution.py:907
  141.2 0.7 copy-start.8
  141.9 25.1 %copy-start.6 = (bf16[2,1,197,768]{3,0,2,1:T(2,128)(2,1)S(1)}, bf16[2,1,197,768]{3,0,2,1:T(2,128)(2,1)}, u32[]{:S(2)}) copy-start(bf16[2,1,197,768]{3,0,2,1:T(2,128)(2,1)} %param.11) | copy-start | bytes 1815556
  161.4 11.9 %collective-permute-start.1 = (bf16[208,768]{1,0:T(8,128)(2,1)}, bf16[208,768]{1,0:T(8,128)(2,1)S(1)}, u32[]{:S(2)}, u32[]{:S(2)}) collective-permute-start(bf16[208,768]{1,0:T(8,128)(2,1)} %get-tuple-element.90), channel_id=1, source_target_pairs={{0,64},{1,65},{2,66},{3,67},{4,68},{5,69},{6,70},{7,71},{8,72},{9,... | collective-permute-start | bytes 958472 | tf_op jit(solution)/shard_map/ppermute | solution.py:907
  173.3 0.7 copy-start.7
  221.0 11.0 %collective-permute-start.2 = (bf16[208,768]{1,0:T(8,128)(2,1)}, bf16[208,768]{1,0:T(8,128)(2,1)S(1)}, u32[]{:S(2)}, u32[]{:S(2)}) collective-permute-start(bf16[208,768]{1,0:T(8,128)(2,1)} %get-tuple-element.110), channel_id=1, source_target_pairs={{64,0},{65,1},{66,2},{67,3},{68,4},{69,5},{70,6},{71,7},{72,8},{73... | collective-permute-start | bytes 958472 | tf_op jit(solution)/shard_map/ppermute | solution.py:907
  231.9 0.7 copy-start.10
  232.7 33.4 %copy-start.1 = (bf16[2,197,768]{2,1,0:T(8,128)(2,1)S(1)}, bf16[2,197,768]{2,1,0:T(8,128)(2,1)}, u32[]{:S(2)}) copy-start(bf16[2,197,768]{2,1,0:T(8,128)(2,1)} %get-tuple-element.103) | copy-start | bytes 1815556
  263.9 10.0 %collective-permute-start.3 = (bf16[208,768]{1,0:T(8,128)(2,1)}, bf16[208,768]{1,0:T(8,128)(2,1)S(1)}, u32[]{:S(2)}, u32[]{:S(2)}) collective-permute-start(bf16[208,768]{1,0:T(8,128)(2,1)} %get-tuple-element.118), channel_id=1, source_target_pairs={{64,0},{65,1},{66,2},{67,3},{68,4},{69,5},{70,6},{71,7},{72,8},{73... | collective-permute-start | bytes 958472 | tf_op jit(solution)/shard_map/ppermute | solution.py:907
  274.0 0.7 copy-start.9
  463.9 3.4 copy-start.3
  467.3 2.9 copy-start

commit v3 on v2

--- a/solution.py
+++ b/solution.py
@@ -61,12 +61,13 @@
     local = pltpu.make_async_copy(own, out.at[xl, z, c], loc)
     local.start()
     mine = quarter(y)
-    first = pl.ds(0, p_rows)
-    plo, pup = pl.ds(0, halves(p_rows)[0]), pl.ds(halves(p_rows)[0], halves(p_rows)[1])
+    first, plo, pup = pl.ds(0, 128), pl.ds(0, 64), pl.ds(64, 64)
+    cross, clo, cup = pl.ds(128, 80), pl.ds(128, 32), pl.ds(160, 48)
     def from_own(rows, dev):
         return go(own.at[rows], block(xl, z, rows), dev)
     q_up, q_down, q_over = from_own(mine, du), from_own(mine, dd), from_own(mine, dx)
     p_over = from_own(first, dx)
+    c_up, c_down, c_over = from_own(cross, du), from_own(cross, dd), from_own(cross, dx)
     p_up, p_down = from_own(first, du), from_own(first, dd)
     q_over.wait_recv()
     q_over_up, q_over_down = pass_on(ox, z, mine, du), pass_on(ox, z, mine, dd)
@@ -88,6 +89,14 @@
     q_over_down.wait_recv()
     f4 = pass_on(ox, zu, upper(y), dd)
     over_y(ox, zu)
+    c_up.wait_recv()
+    h1 = pass_on(xl, zd, clo, du)
+    overs = [c_over, pass_on(xl, zd, cross, dx)]
+    c_down.wait_recv()
+    h2 = pass_on(xl, zu, cup, dd)
+    overs.append(pass_on(xl, zu, cross, dx))
+    share(xl, zd, cross)
+    share(xl, zu, cross)
     p_over.wait_recv()
     p_over_up, p_over_down = pass_on(ox, z, first, du), pass_on(ox, z, first, dd)
     f1.wait_recv()
@@ -96,6 +105,10 @@
     f3.wait_recv()
     f4.wait_recv()
     over_y(ox, zo)
+    h1.wait_recv()
+    h2.wait_recv()
+    overs.append(pass_on(xl, zo, cross, dx))
+    share(xl, zo, cross)
     for a, b in ((xl, zd), (xl, zu), (ox, zd), (ox, zu), (xl, zo), (ox, zo)):
         share(a, b, mine)
     p_up.wait_recv()
@@ -124,8 +137,11 @@
     share(ox, zu, first)
     for item in spread[2:]:
         y_forward(item)
-    for cp in rest_over:
+    for cp in rest_over + overs:
         cp.wait_recv()
+    share(ox, zd, cross)
+    share(ox, zu, cross)
+    share(ox, zo, cross)
     share(ox, z, pl.ds(0, p_rows + q_rows))
     for cp in (g1, g2, g3, g4):
         cp.wait_recv()
@@ -144,7 +160,7 @@
 
 def gather(own, p_rows, core=True, cid=0):
     r, w = own.shape
-    nmax = 80
+    nmax = 110
     def body(own_ref, out_ref, send, recv, loc):
         gather_kernel(p_rows, r - p_rows, core, own_ref, out_ref, send, recv, loc)
     return pl.pallas_call(
@@ -157,7 +173,7 @@
     )(own)
 
 
-def reduce_kernel(gexp, gden, out, acc, rc, ryh, ryf, rzh, rzf, rx, rfh, rff, tfh, tff, small, send, recv, loc):
+def reduce_kernel(gexp, gden, out, acc, rc, ryh, ryf, rzh, rzf, rx, rfh, rff, tfh, tff, rxx, rch, rcf, small, send, recv, loc):
     xl, z, c, y = place()
     ox, zu, zd, zo = 1 - xl, (z + 1) % 4, (z + 3) % 4, (z + 2) % 4
     yu, yd, yo = (y + 1) % 4, (y + 3) % 4, (y + 2) % 4
@@ -212,6 +228,7 @@
         return acc.at[a, b, rows(at, n)]
 
     y_half, y_full, z_half, z_full = {}, {}, {}, {}
+    cross = []
     for t in range(6):
         own_sum(t)
         y_half[t] = (
@@ -220,9 +237,17 @@
         )
         if t < 2:
             z_half[t, 0] = (
-                go(piece(t, 0, 96), rzh.at[t, 0, pl.ds(0, 96)], du),
-                go(piece(t, 96, 112), rzh.at[t, 1, pl.ds(0, 112)], dd),
+                go(piece(t, 0, 64), rzh.at[t, 0, pl.ds(0, 64)], du),
+                go(piece(t, 64, 64), rzh.at[t, 1, pl.ds(0, 64)], dd),
             )
+        if t % 2 == 0:
+            cross.append(go(piece(t, 128, 80), rxx.at[t // 2], dx))
+    cross[0].wait_recv()
+    add(acc.at[xl, zo], 128, rxx.at[0], 0, 80)
+    c_half = (
+        go(piece(1, 128, 32), rch.at[0, pl.ds(0, 32)], du),
+        go(piece(1, 160, 48), rch.at[1], dd),
+    )
     for t in range(6):
         a, b = blocks[t]
         y_half[t][0].wait_recv()
@@ -234,13 +259,27 @@
         if t == 1:
             for x in range(2):
                 z_half[x, 0][0].wait_recv()
-                add(acc.at[blocks[x][0], zu], 0, rzh.at[x, 0], 0, 96)
-                up = go(piece(2 + x, 0, 208), rzf.at[x, 0, pl.ds(0, 208)], du)
+                add(acc.at[blocks[x][0], zu], 0, rzh.at[x, 0], 0, 64)
+                up = go(piece(2 + x, 0, 128), rzf.at[x, 0, pl.ds(0, 128)], du)
                 z_half[x, 0][1].wait_recv()
-                add(acc.at[blocks[x][0], zd], 96, rzh.at[x, 1], 0, 112)
-                z_full[x, 0] = (up, go(piece(4 + x, 0, 208), rzf.at[x, 1, pl.ds(0, 208)], dd))
-    own_sum(6)
-    early = [go(acc.at[ox, z, rows(quarter(k), 64)], rx.at[rows(quarter(k), 64)], dx) for k in (yu, yd, yo)]
+                add(acc.at[blocks[x][0], zd], 64, rzh.at[x, 1], 0, 64)
+                z_full[x, 0] = (up, go(piece(4 + x, 0, 128), rzf.at[x, 1, pl.ds(0, 128)], dd))
+        if t == 2:
+            own_sum(6)
+            early = [
+                go(acc.at[ox, z, rows(quarter(k), 64)], rx.at[rows(quarter(k), 64)], dx) for k in (yu, yd, yo)
+            ]
+            cross.append(go(piece(6, 128, 80), rxx.at[3], dx))
+        if t == 3:
+            for n, b_at in ((1, zu), (2, zd)):
+                cross[n].wait_recv()
+                add(acc.at[xl, b_at], 128, rxx.at[n], 0, 80)
+            c_half[0].wait_recv()
+            add(acc.at[xl, zu], 128, rch.at[0], 0, 32)
+            c_full_up = go(piece(3, 128, 80), rcf.at[0], du)
+            c_half[1].wait_recv()
+            add(acc.at[xl, zd], 160, rch.at[1], 0, 48)
+            c_full = (c_full_up, go(piece(5, 128, 80), rcf.at[1], dd))
     own_sum(7)
     for t in range(6):
         a, b = blocks[t]
@@ -301,9 +340,9 @@
     for x in range(2):
         for side in range(2):
             z_full[x, 0][side].wait_recv()
-            add(acc.at[blocks[x][0], z], 0, rzf.at[x, side], 0, 208)
+            add(acc.at[blocks[x][0], z], 0, rzf.at[x, side], 0, 128)
         if x == 0:
-            over.append(go(acc.at[ox, z, pl.ds(0, 208)], rx.at[pl.ds(0, 208)], dx))
+            over.append(go(acc.at[ox, z, pl.ds(0, 128)], rx.at[pl.ds(0, 128)], dx))
         z_half[x, 1][0].wait_recv()
         add(acc.at[blocks[x][0], zu], quarter(y), rzh.at[x, 0], 112, 32)
         up = go(piece(2 + x, quarter(y), 64), rzf.at[x, 0, pl.ds(208, 64)], du)
@@ -320,7 +359,12 @@
         if x == 0:
             over.append(go(acc.at[ox, z, rows(quarter(y), 64)], rx.at[rows(quarter(y), 64)], dx))
             over[0].wait_recv()
-            add(own, 0, rx, 0, 208)
+            add(own, 0, rx, 0, 128)
+            cross[3].wait_recv()
+            add(own, 128, rxx.at[3], 0, 80)
+            for side in range(2):
+                c_full[side].wait_recv()
+                add(own, 128, rcf.at[side], 0, 80)
             keep = load(own.at[tail], small.at[y])
             tails = [go(own.at[tail], small.at[y], d) for d in (dyu, dyd, dyo)]
             next(end_one)
@@ -372,6 +416,9 @@
             pltpu.VMEM((2, 64, w), low),
             pltpu.VMEM((2, 32, w), low),
             pltpu.VMEM((2, 48, w), low),
+            pltpu.VMEM((4, 80, w), low),
+            pltpu.VMEM((2, 48, w), low),
+            pltpu.VMEM((2, 80, w), low),
             pltpu.VMEM((4, 16, w), low),
             pltpu.SemaphoreType.DMA((n,)),
             pltpu.SemaphoreType.DMA((n,)),
@@ -886,15 +933,15 @@
 def spread_kernel(total, g_in, g_out, g_qkv, g_proj, small):
     for e in range(3):
         cols = pl.ds(e * 768, 768)
-        g_in[0, :, e, :] = total[pl.ds(80, 192), cols].astype(F32)
-        g_out[0, :, e, :] = total[pl.ds(272, 192), cols].astype(F32)
+        g_in[0, e] = total[pl.ds(80, 192), cols].astype(F32)
+        g_out[0, e] = total[pl.ds(272, 192), cols].astype(F32)
         g_proj[0, pl.ds(e * 16, 16), :] = total[pl.ds(16, 16), cols].astype(F32)
     g_qkv[0] = total[pl.ds(32, 48), :].astype(F32)
     small[...] = total[pl.ds(0, 16), pl.ds(0, 768)].astype(F32)
 
 
 def spread(total):
-    shapes = [(1, 192, 3, 768), (1, 192, 3, 768), (1, 48, 2304), (1, 48, 768), (16, 768)]
+    shapes = [(1, 3, 192, 768), (1, 3, 192, 768), (1, 48, 2304), (1, 48, 768), (16, 768)]
     return pl.pallas_call(
         spread_kernel,
         out_shape=[jax.ShapeDtypeStruct(shape, F32) for shape in shapes],
@@ -902,9 +949,25 @@
     )(total)
 
 
-def to_section(value, by):
-    pairs = [(i, i + by) for i in range(2) if 0 <= i + by < 2]
-    return lax.ppermute(value, "section", pairs)
+def hop_kernel(value, out, send, recv):
+    peer = {"section": 1 - lax.axis_index("section")}
+    greet([peer])
+    cp = pltpu.make_async_remote_copy(
+        src_ref=value, dst_ref=out, send_sem=send, recv_sem=recv, device_id=peer, device_id_type=MESH
+    )
+    cp.start()
+    cp.wait()
+
+
+def swap_sections(value):
+    return pl.pallas_call(
+        hop_kernel,
+        out_shape=jax.ShapeDtypeStruct(value.shape, value.dtype),
+        in_specs=[pl.BlockSpec(memory_space=pl.ANY)],
+        out_specs=pl.BlockSpec(memory_space=pl.ANY),
+        scratch_shapes=[pltpu.SemaphoreType.DMA(()), pltpu.SemaphoreType.DMA(())],
+        compiler_params=pltpu.CompilerParams(collective_id=2, has_side_effects=True),
+    )(value)
 
 
 def local(
@@ -914,8 +977,8 @@
     small = jnp.concatenate([w_router[0], norm_gain[0].T, norm_offset[0].T], axis=1)
     own = jnp.concatenate(
         [
-            experts_in[0].reshape(192, 2304),
-            experts_out[0].reshape(192, 2304),
+            jnp.concatenate([experts_in[0, :, e] for e in range(3)], axis=1),
+            jnp.concatenate([experts_out[0, :, e] for e in range(3)], axis=1),
             w_qkv[0],
             w_proj[0].reshape(3, 16, 768).transpose(1, 0, 2).reshape(16, 2304),
             jnp.pad(small.reshape(16, 21), ((0, 0), (0, 2283))),
@@ -936,14 +999,14 @@
         at = jnp.stack([jnp.clip(tick - section, 0, 1), section]).astype(jnp.int32)
         sent, caches = forward_tick(at, inputs, received, routes, every, router, norms, caches)
         if tick < 2:
-            received = to_section(sent, 1)
+            received = swap_sections(sent)
     returned = jnp.zeros((TOKENS, 768), LOW)
     backs = None
     for tick in range(3):
         at = jnp.stack([jnp.clip(tick - 1 + section, 0, 1), section]).astype(jnp.int32)
         sent, backs = backward_tick(at, cotangent, returned, routes, every, router, norms, caches, backs)
         if tick < 2:
-            returned = to_section(sent, -1)
+            returned = swap_sections(sent)
     gexp, gden = weight_grads(caches, backs)
     total = reduce_grads(gexp.reshape(2, 4, 2, 384, 2304), gden.reshape(2, 4, 2, 80, 2304))
     g_in, g_out, g_qkv, g_proj, small = spread(total)
@@ -956,8 +1019,8 @@
         g_qkv,
         g_proj,
         mine[:3].T[None],
-        g_in,
-        g_out,
+        g_in.transpose(0, 2, 1, 3),
+        g_out.transpose(0, 2, 1, 3),
     )
 
 

time: 482 us -> 456 us (0.946)
  waiting for transfers between devices: 26.2 us -> 0 us
  Pallas kernels: 404 us -> 429 us
  starting transfers between devices: 13.4 us -> 0 us
  local copies, waits for them, and re-layouts: 25.6 us -> 17.7 us
    pallas_call x0 -> x4, Pallas kernels: none -> 39 us  [swap_sections(): pl.pallas_call(hop_kernel, out_shape=jax.ShapeDtypeStruct(value.shape, va...]
    ppermute x4 -> x0, waiting for transfers between devices: 26.2 us -> none  [to_section(): return lax.ppermute(value, 'section', pairs)]
    ppermute x4 -> x0, starting transfers between devices: 13.4 us -> none  [to_section(): return lax.ppermute(value, 'section', pairs)]
    unnamed x52 -> x30, local copies, waits for them, and re-layouts: 18.1 us -> 10.1 us
    pallas_call x1, Pallas kernels: 133 us -> 125 us  [reduce_grads(): pl.pallas_call(reduce_kernel, out_shape=jax.ShapeDtypeStruct((464, w), lo...]
    pallas_call x1, Pallas kernels: 97.2 us -> 91.9 us  [gather(): pl.pallas_call(body, out_shape=jax.ShapeDtypeStruct((2, 4, 2, r, w), own....]
  transfers between devices with their start and end apart: 4 -> 0, of which waited for: 4 -> 0; matrix products, arithmetic and copies ran while one was open for 1% -> 0% of each run, Pallas kernels for 0% -> 0%
where the time goes in v3:
time: 456 us; the launch traced here: 451 us
  Pallas kernels  429 us (94%)
  local copies, waits for them, and re-layouts  17.7 us (4%)
    pallas_call x6, Pallas kernels, call_tick(): pl.pallas_call(body, out_shape=[jax.ShapeDtypeStruct((TOKENS, 768), LOW)]...  149 us
    pallas_call x1, Pallas kernels, reduce_grads(): pl.pallas_call(reduce_kernel, out_shape=jax.ShapeDtypeStruct((464, w), lo...  125 us
    pallas_call x1, Pallas kernels, gather(): pl.pallas_call(body, out_shape=jax.ShapeDtypeStruct((2, 4, 2, r, w), own....  91.9 us
    pallas_call x4, Pallas kernels, swap_sections(): pl.pallas_call(hop_kernel, out_shape=jax.ShapeDtypeStruct(value.shape, va...  39 us
    pallas_call x1, Pallas kernels, weight_grads(): pl.pallas_call(weight_kernel, out_shape=[jax.ShapeDtypeStruct((16, 384, 2...  21.2 us
    unnamed x30, local copies, waits for them, and re-layouts  10.1 us

profile of v3, /device:TPU:1, one launch (start us, length us, event | category | flops | bytes accessed | tf_op | source)
XLA Modules:
  0.0 450.9 jit_solution(6905040018535185330)
XLA Ops:
  1.3 1.1 copy.85
  2.4 0.9 pad.25.inputs
  6.3 1.3 copy-done
  7.6 91.9 %shard_map.169 = bf16[2,4,2,464,2304]{4,3,2,1,0:T(8,128)(2,1)} custom-call(bf16[464,2304]{1,0:T(8,128)(2,1)} %copy-done), custom_call_target="tpu_custom_call" | custom-call | tf_op jit(solution)/shard_map/pallas_call | solution.py:166
  99.5 0.9 slice.48
  102.1 0.7 broadcast_1_received_returned.2.received.returned
  102.8 20.0 %shard_map.170 = (bf16[208,768]{1,0:T(8,128)(2,1)}, bf16[2,197,768]{2,1,0:T(8,128)(2,1)}, bf16[2,208,768]{2,1,0:T(8,128)(2,1)}, bf16[2,208,768]{2,1,0:T(8,128)(2...) custom-call(s32[2]{0:T(128)} %get-tuple-element.173.at, ...), custom_call_target="tpu_custom_call" | custom-call | flops 4000000000 | bytes 40000000 | tf_op jit(solution)/shard_map/pallas_call | solution.py:685
  122.8 11.1 %shard_map.171.received = bf16[208,768]{1,0:T(8,128)(2,1)} custom-call(bf16[208,768]{1,0:T(8,128)(2,1)} %get-tuple-element.77.value), custom_call_target="tpu_custom_call" | custom-call | tf_op jit(solution)/shard_map/pallas_call | solution.py:963
  133.9 19.4 %shard_map.172 = (bf16[208,768]{1,0:T(8,128)(2,1)}, bf16[2,197,768]{2,1,0:T(8,128)(2,1)}, bf16[2,208,768]{2,1,0:T(8,128)(2,1)}, bf16[2,208,768]{2,1,0:T(8,128)(2...) custom-call(s32[2]{0:T(128)} %get-tuple-element.172.at, ...), custom_call_target="tpu_custom_call", output_to_operand_aliasing={{1}: (7, {}), {2}: (8, {}), {3}: (9, {}), {4}: (10, {}), {5... | custom-call | flops 4000000000 | bytes 40000000 | tf_op jit(solution)/shard_map/pallas_call | solution.py:685
  153.3 10.2 %shard_map.173.received = bf16[208,768]{1,0:T(8,128)(2,1)} custom-call(bf16[208,768]{1,0:T(8,128)(2,1)} %get-tuple-element.90.value), custom_call_target="tpu_custom_call" | custom-call | tf_op jit(solution)/shard_map/pallas_call | solution.py:963
  163.6 19.7 %shard_map.174 = (bf16[208,768]{1,0:T(8,128)(2,1)}, bf16[2,197,768]{2,1,0:T(8,128)(2,1)}, bf16[2,208,768]{2,1,0:T(8,128)(2,1)}, bf16[2,208,768]{2,1,0:T(8,128)(2...) custom-call(s32[2]{0:T(128)} %get-tuple-element.171.at, ...), custom_call_target="tpu_custom_call", output_to_operand_aliasing={{1}: (7, {}), {2}: (8, {}), {3}: (9, {}), {4}: (10, {}), {5... | custom-call | flops 4000000000 | bytes 40000000 | tf_op jit(solution)/shard_map/pallas_call | solution.py:685
  183.3 2.4 copy.77
  185.7 0.9 pad.31.cotangent
  187.3 27.1 %shard_map.175 = (bf16[208,768]{1,0:T(8,128)(2,1)}, f32[2,197,768]{2,1,0:T(8,128)}, bf16[2,256,768]{2,1,0:T(8,128)(2,1)}, bf16[2,240,3072]{2,1,0:T(8,128)(2,1)},...) custom-call(s32[2]{0:T(128)} %get-tuple-element.176.at, ...), custom_call_target="tpu_custom_call" | custom-call | flops 6000000000 | bytes 40000000 | tf_op jit(solution)/shard_map/pallas_call | solution.py:685
  214.4 9.3 %shard_map.176.returned = bf16[208,768]{1,0:T(8,128)(2,1)} custom-call(bf16[208,768]{1,0:T(8,128)(2,1)} %get-tuple-element.110.value), custom_call_target="tpu_custom_call" | custom-call | tf_op jit(solution)/shard_map/pallas_call | solution.py:963
  223.7 31.3 %shard_map.177 = (bf16[208,768]{1,0:T(8,128)(2,1)}, f32[2,197,768]{2,1,0:T(8,128)}, bf16[2,256,768]{2,1,0:T(8,128)(2,1)}, bf16[2,240,3072]{2,1,0:T(8,128)(2,1)},...) custom-call(s32[2]{0:T(128)} %get-tuple-element.175.at, ...), custom_call_target="tpu_custom_call", output_to_operand_aliasing={{1}: (13, {}), {2}: (14, {}), {3}: (15, {}), {4}: (16, {}),... | custom-call | flops 6000000000 | bytes 40000000 | tf_op jit(solution)/shard_map/pallas_call | solution.py:685
  255.0 8.4 %shard_map.178.returned = bf16[208,768]{1,0:T(8,128)(2,1)} custom-call(bf16[208,768]{1,0:T(8,128)(2,1)} %get-tuple-element.118.value), custom_call_target="tpu_custom_call" | custom-call | tf_op jit(solution)/shard_map/pallas_call | solution.py:963
  263.4 31.5 %shard_map.179 = (bf16[208,768]{1,0:T(8,128)(2,1)}, f32[2,197,768]{2,1,0:T(8,128)}, bf16[2,256,768]{2,1,0:T(8,128)(2,1)}, bf16[2,240,3072]{2,1,0:T(8,128)(2,1)},...) custom-call(s32[2]{0:T(128)} %get-tuple-element.174.at, ...), custom_call_target="tpu_custom_call", output_to_operand_aliasing={{1}: (13, {}), {2}: (14, {}), {3}: (15, {}), {4}: (16, {}),... | custom-call | flops 6000000000 | bytes 40000000 | tf_op jit(solution)/shard_map/pallas_call | solution.py:685
  294.9 3.6 copy.78
  298.5 21.2 %shard_map.180 = (bf16[16,384,2304]{2,1,0:T(8,128)(2,1)}, bf16[16,80,2304]{2,1,0:T(8,128)(2,1)}) custom-call(bf16[2,208,768]{2,1,0:T(8,128)(2,1)} %get-tuple-element.127.c_nin, bf16[2,208,768]{2,1,0:T(8,128)(2,1)} %get-tuple-element.128.c_mix, bf16[2,208,768]{2,1,0:T(8,128)(2,1)} %get-tuple-element.129.c_nrm, ...), custom_call_target="tpu_custom_call" | custom-call | tf_op jit(solution)/shard_map/pallas_call | solution.py:916
  319.7 124.6 %shard_map.181.total = bf16[464,2304]{1,0:T(8,128)(2,1)} custom-call(bf16[2,4,2,384,2304]{4,3,2,1,0:T(8,128)(2,1)} %bitcast.63, bf16[2,4,2,80,2304]{4,3,2,1,0:T(8,128)(2,1)} %bitcast.65), custom_call_target="tpu_custom_call" | custom-call | tf_op jit(solution)/shard_map/pallas_call | solution.py:402
  444.3 3.7 shard_map.182
  448.0 1.4 dynamic-slice_bitcast_fusion.1
  449.4 0.8 dynamic-slice_bitcast_fusion
  (43 shorter events, 6.5 us)
Async XLA Ops:
  0.6 3.3 copy-start.6
  0.7 4.1 copy-start.1
  3.3 1.6 copy-start.2
  4.9 0.9 copy-start.4
  4.9 1.0 copy-start.5
  4.9 1.1 copy-start.7
  4.9 1.1 copy-start.8
  4.9 1.1 copy-start.9
  6.2 1.3 copy-start
  163.6 22.1 %copy-start.3 = (bf16[2,1,197,768]{3,0,2,1:T(2,128)(2,1)S(1)}, bf16[2,1,197,768]{3,0,2,1:T(2,128)(2,1)}, u32[]{:S(2)}) copy-start(bf16[2,1,197,768]{3,0,2,1:T(2,128)(2,1)} %param.11) | copy-start | bytes 1815556

commit v4 on v3

--- a/solution.py
+++ b/solution.py
@@ -1,3 +1,5 @@
+import functools
+
 import jax
 import jax.numpy as jnp
 from jax import lax
@@ -554,12 +556,12 @@
     ]
 
 
-def forward_kernel(at, inputs, received, routes, every, router, norms, *rest):
+def forward_kernel(pick, at, inputs, received, routes, every, router, norms, *rest):
     sent, section_out, *outs = rest[-31:-18]
     (u_at, nin, pro, mix, res, nrm, gate, slot, pre_at, hid, result_at,
      wp, acc, experts, qkv, proj, sems, out_sems) = rest[-18:]
     kept = [u_at, nin, pro, mix, res, nrm, gate, slot, pre_at, hid, result_at]
-    micro = at[0]
+    micro = pick(at)
     weights = Weights(every, experts, qkv, proj, sems)
     weights.start_dense()
     weights.start_chunks()
@@ -567,7 +569,13 @@
     def save(n):
         return pltpu.make_async_copy(kept[n], outs[n].at[micro], out_sems.at[n])
 
-    u_low = jnp.where(at[1] == 0, inputs[0], received[...])
+    def save_part(n, j):
+        cols = columns_of(j)
+        return pltpu.make_async_copy(
+            kept[n].at[:, cols], outs[n].at[micro, :, cols], out_sems.at[12 + (n - 8) * STEPS + j]
+        )
+
+    u_low = jnp.where(at[0] == 0, inputs[0], received[...])
     u_at[...] = u_low
     save(0).start()
     u = u_low.astype(F32)
@@ -617,15 +625,15 @@
         for e in range(3):
             rows = slots_of(e)
             pre = mm(slot[rows, :], weights.block(j, 0, e), NT)
-            pre_at[rows, cols] = pre
+            pre_at[rows, cols] = pre.astype(LOW)
             hidden = (0.5 * pre * (1.0 + tanh_part(pre))).astype(LOW)
             hid[rows, cols] = hidden
             acc[rows, :] += mm(hidden, weights.block(j, 1, e))
+        save_part(8, j).start()
+        save_part(9, j).start()
         return carry
 
     lax.fori_loop(0, STEPS, step, 0)
-    save(8).start()
-    save(9).start()
     result = acc[...].astype(LOW)
     result_at[...] = result
     save(10).start()
@@ -635,16 +643,19 @@
     y = y.astype(LOW)
     sent[...] = y
     section_out[0] = y[:197]
-    for n in range(11):
+    for n in (0, 1, 2, 3, 4, 5, 6, 7, 10):
         save(n).wait()
+    for j in range(STEPS):
+        save_part(8, j).wait()
+        save_part(9, j).wait()
 
 
 def whole(shape):
     return pl.BlockSpec(shape, lambda j, at: (0,) * len(shape))
 
 
-def by_micro(shape):
-    return pl.BlockSpec((1,) + shape[1:], lambda j, at: (at[0],) + (0,) * (len(shape) - 1))
+def by_micro(shape, pick):
+    return pl.BlockSpec((1,) + shape[1:], lambda j, at: (pick(at),) + (0,) * (len(shape) - 1))
 
 
 ANYWHERE = pl.BlockSpec(memory_space=pl.ANY)
@@ -658,7 +669,7 @@
     ((2, TOKENS, 768), LOW),
     ((2, TOKENS, LANES), F32),
     ((2, 256, 768), LOW),
-    ((2, 3 * SLOT_ROWS, 3072), F32),
+    ((2, 3 * SLOT_ROWS, 3072), LOW),
     ((2, 3 * SLOT_ROWS, 3072), LOW),
     ((2, 256, 768), LOW),
 ]
@@ -673,7 +684,7 @@
 ]
 
 
-def call_tick(body, at, operands, specs, kept, kinds, scratch, flops):
+def call_tick(body, pick, at, operands, specs, kept, kinds, scratch, flops):
     grown = list(operands)
     grown_specs = list(specs)
     aliases = {}
@@ -683,18 +694,18 @@
             grown.append(array)
             grown_specs.append(ANYWHERE)
     return pl.pallas_call(
-        body,
+        functools.partial(body, pick),
         out_shape=[jax.ShapeDtypeStruct((TOKENS, 768), LOW)]
         + [jax.ShapeDtypeStruct(shape, kind) for shape, kind in kinds],
         grid_spec=pltpu.PrefetchScalarGridSpec(
             num_scalar_prefetch=1,
             grid=(1,),
             in_specs=grown_specs,
-            out_specs=[whole((TOKENS, 768)), by_micro(kinds[0][0])] + [ANYWHERE] * (len(kinds) - 1),
+            out_specs=[whole((TOKENS, 768)), by_micro(kinds[0][0], pick)] + [ANYWHERE] * (len(kinds) - 1),
             scratch_shapes=[pltpu.VMEM(shape[1:], kind) for shape, kind in kinds[1:]]
             + scratch
             + weight_scratch()
-            + [pltpu.SemaphoreType.DMA((len(kinds),))],
+            + [pltpu.SemaphoreType.DMA((len(kinds) + 2 * STEPS,))],
         ),
         input_output_aliases=aliases,
         compiler_params=pltpu.CompilerParams(vmem_limit_bytes=60 * 1024 * 1024),
@@ -702,13 +713,14 @@
     )(at, *grown)
 
 
-def forward_tick(at, inputs, received, routes, every, router, norms, kept):
+def forward_tick(pick, at, inputs, received, routes, every, router, norms, kept):
     outs = call_tick(
         forward_kernel,
+        pick,
         at,
         [inputs, received, routes, every, router, norms],
         [
-            by_micro(inputs.shape), whole((TOKENS, 768)), by_micro(routes.shape), ANYWHERE,
+            by_micro(inputs.shape, pick), whole((TOKENS, 768)), by_micro(routes.shape, pick), ANYWHERE,
             whole(router.shape), whole(norms.shape),
         ],
         kept,
@@ -720,13 +732,13 @@
 
 
 def backward_kernel(
-    at, cotangent, returned, routes, every, router, norms, gate, result, h_u, h_pro, h_res, h_pre, *rest
+    pick, at, cotangent, returned, routes, every, router, norms, gate, result, h_u, h_pro, h_res, h_pre, *rest
 ):
     sent, section_in_grad, *outs = rest[-26:-18]
     (gres, gpre, ga_at, gp, gl, gnorm,
      wp, acc, u_at, pro, res, pre_at, in_sems, experts, qkv, proj, sems, out_sems) = rest[-18:]
     kept = [gres, gpre, ga_at, gp, gl, gnorm]
-    micro = at[0]
+    micro = pick(at)
     weights = Weights(every, experts, qkv, proj, sems)
     sources, targets = (h_pre, h_res, h_pro, h_u), (pre_at, res, pro, u_at)
 
@@ -741,7 +753,7 @@
     weights.start_dense()
     for n in range(1, 4):
         fetch(n).start()
-    gy = jnp.where(at[1] == 1, cotangent[0], returned[...]).astype(F32)
+    gy = jnp.where(at[0] == 1, cotangent[0], returned[...]).astype(F32)
     one, two, hot_one, hot_two = route_tables(routes[0])
     gates = gate[0]
     gate_one = jnp.sum(gates * hot_one, axis=1, keepdims=True)
@@ -767,7 +779,7 @@
         for e in range(3):
             rows = slots_of(e)
             grad_hidden = mm(gres[rows, :], weights.block(j, 1, e), NT)
-            x = pre_at[rows, cols]
+            x = pre_at[rows, cols].astype(F32)
             t = tanh_part(x)
             slope = 0.5 * (1.0 + t) + 0.5 * x * (1.0 - t * t) * (
                 0.7978845608028654 * (1.0 + 3 * 0.044715 * (x * x))
@@ -832,15 +844,16 @@
         save(n).wait()
 
 
-def backward_tick(at, cotangent, returned, routes, every, router, norms, caches, kept):
+def backward_tick(pick, at, cotangent, returned, routes, every, router, norms, caches, kept):
     _, c_u, _, c_pro, _, c_res, _, c_gate, _, c_pre, _, c_result = caches
     outs = call_tick(
         backward_kernel,
+        pick,
         at,
         [cotangent, returned, routes, every, router, norms, c_gate, c_result, c_u, c_pro, c_res, c_pre],
         [
-            by_micro(cotangent.shape), whole((TOKENS, 768)), by_micro(routes.shape), ANYWHERE,
-            whole(router.shape), whole(norms.shape), by_micro(c_gate.shape), by_micro(c_result.shape),
+            by_micro(cotangent.shape, pick), whole((TOKENS, 768)), by_micro(routes.shape, pick), ANYWHERE,
+            whole(router.shape), whole(norms.shape), by_micro(c_gate.shape, pick), by_micro(c_result.shape, pick),
         ]
         + [ANYWHERE] * 4,
         kept,
@@ -973,7 +986,9 @@
 def local(
     inputs, cotangent, routes, norm_gain, norm_offset, w_qkv, w_proj, w_router, experts_in, experts_out
 ):
-    section = lax.axis_index("section")
+    at = lax.axis_index("section").astype(jnp.int32).reshape(1)
+    ahead = (lambda at: 0, lambda at: 1 - at[0], lambda at: 1)
+    back = (lambda at: 0, lambda at: at[0], lambda at: 1)
     small = jnp.concatenate([w_router[0], norm_gain[0].T, norm_offset[0].T], axis=1)
     own = jnp.concatenate(
         [
@@ -996,15 +1011,13 @@
     received = jnp.zeros((TOKENS, 768), LOW)
     caches = None
     for tick in range(3):
-        at = jnp.stack([jnp.clip(tick - section, 0, 1), section]).astype(jnp.int32)
-        sent, caches = forward_tick(at, inputs, received, routes, every, router, norms, caches)
+        sent, caches = forward_tick(ahead[tick], at, inputs, received, routes, every, router, norms, caches)
         if tick < 2:
             received = swap_sections(sent)
     returned = jnp.zeros((TOKENS, 768), LOW)
     backs = None
     for tick in range(3):
-        at = jnp.stack([jnp.clip(tick - 1 + section, 0, 1), section]).astype(jnp.int32)
-        sent, backs = backward_tick(at, cotangent, returned, routes, every, router, norms, caches, backs)
+        sent, backs = backward_tick(back[tick], at, cotangent, returned, routes, every, router, norms, caches, backs)
         if tick < 2:
             returned = swap_sections(sent)
     gexp, gden = weight_grads(caches, backs)

time: 456 us -> 439 us (0.963)
  Pallas kernels: 429 us -> 414 us
    pallas_call x6, Pallas kernels: 149 us -> 134 us  [call_tick(): pl.pallas_call(functools.partial(body, pick), out_shape=[jax.ShapeDtypeSt...]
where the time goes in v4:
time: 439 us; the launch traced here: 434 us
  Pallas kernels  414 us (94%)
  local copies, waits for them, and re-layouts  18.1 us (4%)
    pallas_call x6, Pallas kernels, call_tick(): pl.pallas_call(functools.partial(body, pick), out_shape=[jax.ShapeDtypeSt...  134 us
    pallas_call x1, Pallas kernels, reduce_grads(): pl.pallas_call(reduce_kernel, out_shape=jax.ShapeDtypeStruct((464, w), lo...  124 us
    pallas_call x1, Pallas kernels, gather(): pl.pallas_call(body, out_shape=jax.ShapeDtypeStruct((2, 4, 2, r, w), own....  91.9 us
    pallas_call x4, Pallas kernels, swap_sections(): pl.pallas_call(hop_kernel, out_shape=jax.ShapeDtypeStruct(value.shape, va...  38.9 us
    pallas_call x1, Pallas kernels, weight_grads(): pl.pallas_call(weight_kernel, out_shape=[jax.ShapeDtypeStruct((16, 384, 2...  21.2 us
    unnamed x30, local copies, waits for them, and re-layouts  10.5 us

profile of v4, /device:TPU:1, one launch (start us, length us, event | category | flops | bytes accessed | tf_op | source)
XLA Modules:
  0.0 433.7 jit_solution(13340976711402978576)
XLA Ops:
  0.7 1.2 copy.85
  1.9 0.9 pad.25.inputs
  4.2 0.8 copy-done.4
  5.4 1.3 copy-done
  6.7 91.9 %shard_map.169 = bf16[2,4,2,464,2304]{4,3,2,1,0:T(8,128)(2,1)} custom-call(bf16[464,2304]{1,0:T(8,128)(2,1)} %copy-done), custom_call_target="tpu_custom_call" | custom-call | tf_op jit(solution)/shard_map/pallas_call | solution.py:168
  98.6 0.9 slice.48
  101.9 18.2 %shard_map.170 = (bf16[208,768]{1,0:T(8,128)(2,1)}, bf16[2,197,768]{2,1,0:T(8,128)(2,1)}, bf16[2,208,768]{2,1,0:T(8,128)(2,1)}, bf16[2,208,768]{2,1,0:T(8,128)(2...) custom-call(s32[1]{0:T(128)} %bitcast.at, ...), custom_call_target="tpu_custom_call" | custom-call | flops 4000000000 | bytes 40000000 | tf_op jit(solution)/shard_map/pallas_call | solution.py:696
  120.2 11.1 %shard_map.171.received = bf16[208,768]{1,0:T(8,128)(2,1)} custom-call(bf16[208,768]{1,0:T(8,128)(2,1)} %get-tuple-element.77.value), custom_call_target="tpu_custom_call" | custom-call | tf_op jit(solution)/shard_map/pallas_call | solution.py:976
  131.3 17.7 %shard_map.172 = (bf16[208,768]{1,0:T(8,128)(2,1)}, bf16[2,197,768]{2,1,0:T(8,128)(2,1)}, bf16[2,208,768]{2,1,0:T(8,128)(2,1)}, bf16[2,208,768]{2,1,0:T(8,128)(2...) custom-call(s32[1]{0:T(128)} %bitcast.at, ...), custom_call_target="tpu_custom_call", output_to_operand_aliasing={{1}: (7, {}), {2}: (8, {}), {3}: (9, {}), {4}: (10, {}), {5... | custom-call | flops 4000000000 | bytes 40000000 | tf_op jit(solution)/shard_map/pallas_call | solution.py:696
  149.0 10.2 %shard_map.173.received = bf16[208,768]{1,0:T(8,128)(2,1)} custom-call(bf16[208,768]{1,0:T(8,128)(2,1)} %get-tuple-element.90.value), custom_call_target="tpu_custom_call" | custom-call | tf_op jit(solution)/shard_map/pallas_call | solution.py:976
  159.2 17.9 %shard_map.174 = (bf16[208,768]{1,0:T(8,128)(2,1)}, bf16[2,197,768]{2,1,0:T(8,128)(2,1)}, bf16[2,208,768]{2,1,0:T(8,128)(2,1)}, bf16[2,208,768]{2,1,0:T(8,128)(2...) custom-call(s32[1]{0:T(128)} %bitcast.at, ...), custom_call_target="tpu_custom_call", output_to_operand_aliasing={{1}: (7, {}), {2}: (8, {}), {3}: (9, {}), {4}: (10, {}), {5... | custom-call | flops 4000000000 | bytes 40000000 | tf_op jit(solution)/shard_map/pallas_call | solution.py:696
  177.1 2.4 copy.77
  179.6 0.9 pad.31.cotangent
  180.5 24.1 %shard_map.175 = (bf16[208,768]{1,0:T(8,128)(2,1)}, f32[2,197,768]{2,1,0:T(8,128)}, bf16[2,256,768]{2,1,0:T(8,128)(2,1)}, bf16[2,240,3072]{2,1,0:T(8,128)(2,1)},...) custom-call(s32[1]{0:T(128)} %bitcast.at, ...), custom_call_target="tpu_custom_call" | custom-call | flops 6000000000 | bytes 40000000 | tf_op jit(solution)/shard_map/pallas_call | solution.py:696
  204.5 9.3 %shard_map.176.returned = bf16[208,768]{1,0:T(8,128)(2,1)} custom-call(bf16[208,768]{1,0:T(8,128)(2,1)} %get-tuple-element.110.value), custom_call_target="tpu_custom_call" | custom-call | tf_op jit(solution)/shard_map/pallas_call | solution.py:976
  213.8 31.3 %shard_map.177 = (bf16[208,768]{1,0:T(8,128)(2,1)}, f32[2,197,768]{2,1,0:T(8,128)}, bf16[2,256,768]{2,1,0:T(8,128)(2,1)}, bf16[2,240,3072]{2,1,0:T(8,128)(2,1)},...) custom-call(s32[1]{0:T(128)} %bitcast.at, ...), custom_call_target="tpu_custom_call", output_to_operand_aliasing={{1}: (13, {}), {2}: (14, {}), {3}: (15, {}), {4}: (16, {}),... | custom-call | flops 6000000000 | bytes 40000000 | tf_op jit(solution)/shard_map/pallas_call | solution.py:696
  245.1 8.3 %shard_map.178.returned = bf16[208,768]{1,0:T(8,128)(2,1)} custom-call(bf16[208,768]{1,0:T(8,128)(2,1)} %get-tuple-element.118.value), custom_call_target="tpu_custom_call" | custom-call | tf_op jit(solution)/shard_map/pallas_call | solution.py:976
  253.5 24.5 %shard_map.179 = (bf16[208,768]{1,0:T(8,128)(2,1)}, f32[2,197,768]{2,1,0:T(8,128)}, bf16[2,256,768]{2,1,0:T(8,128)(2,1)}, bf16[2,240,3072]{2,1,0:T(8,128)(2,1)},...) custom-call(s32[1]{0:T(128)} %bitcast.at, ...), custom_call_target="tpu_custom_call", output_to_operand_aliasing={{1}: (13, {}), {2}: (14, {}), {3}: (15, {}), {4}: (16, {}),... | custom-call | flops 6000000000 | bytes 40000000 | tf_op jit(solution)/shard_map/pallas_call | solution.py:696
  278.0 3.6 copy.78
  281.5 21.2 %shard_map.180 = (bf16[16,384,2304]{2,1,0:T(8,128)(2,1)}, bf16[16,80,2304]{2,1,0:T(8,128)(2,1)}) custom-call(bf16[2,208,768]{2,1,0:T(8,128)(2,1)} %get-tuple-element.127.c_nin, bf16[2,208,768]{2,1,0:T(8,128)(2,1)} %get-tuple-element.128.c_mix, bf16[2,208,768]{2,1,0:T(8,128)(2,1)} %get-tuple-element.129.c_nrm, ...), custom_call_target="tpu_custom_call" | custom-call | tf_op jit(solution)/shard_map/pallas_call | solution.py:929
  302.7 124.4 %shard_map.181.total = bf16[464,2304]{1,0:T(8,128)(2,1)} custom-call(bf16[2,4,2,384,2304]{4,3,2,1,0:T(8,128)(2,1)} %bitcast.57, bf16[2,4,2,80,2304]{4,3,2,1,0:T(8,128)(2,1)} %bitcast.59), custom_call_target="tpu_custom_call" | custom-call | tf_op jit(solution)/shard_map/pallas_call | solution.py:404
  427.1 3.7 shard_map.182
  430.8 1.4 dynamic-slice_bitcast_fusion.1
  432.2 0.8 dynamic-slice_bitcast_fusion
  (40 shorter events, 4.9 us)
Async XLA Ops:
  0.6 2.1 copy-start.6
  0.7 3.0 copy-start.1
  2.8 1.2 copy-start.2
  4.0 0.9 copy-start.4
  4.0 1.0 copy-start.5
  4.0 1.1 copy-start.7
  4.0 1.1 copy-start.8
  4.0 1.1 copy-start.9
  5.3 1.3 copy-start
  159.2 20.3 %copy-start.3 = (bf16[2,1,197,768]{3,0,2,1:T(2,128)(2,1)S(1)}, bf16[2,1,197,768]{3,0,2,1:T(2,128)(2,1)}, u32[]{:S(2)}) copy-start(bf16[2,1,197,768]{3,0,2,1:T(2,128)(2,1)} %param.11) | copy-start | bytes 1815556
